TPU v7x, 32 devices: a whole 2x2x4 slice. The times are simulated.
32 devices in a mesh: sx: 4 (over z), sy: 8 (over y, x, core).
Axes of the slice: x: 2, y: 2, z: 4, core: 2. Of those that a mesh axis runs over, the one named last changes fastest.
Arguments:
- right_side: float32 [128, 128, 128], P('sx', 'sy'), may hold values from -48 to 48
- class_map: int32 [64, 64, 32], P('sx', 'sy'), may hold values from 0 to 7
- conductivity_table: float32 [8], replicated, may hold values from 0.2 to 5
- velocity: float32 [3, 128, 128, 128], P(None, 'sx', 'sy'), may hold values from -6 to 6
Outputs:
- potential: float32 [128, 128, 128], P('sx', 'sy')
- velocity_next: float32 [3, 128, 128, 128], P(None, ('sx', 'sy'))
All inputs are finite; a program needn't handle non-finite values.
Results may differ from a plain program's by a relative error of at most 0.0003.
Values sent between devices are 32-bit elements; how exact they have to be, the bound alone decides.
A program may use at most 64 MiB of HBM per device.

v0:
```python
import jax
import jax.numpy as jnp
from jax import lax
from jax.sharding import PartitionSpec as P

MARGIN = 4
SWEEPS = 5
CLASSES = 8


axial_ratio = 0.0625
coupling = 0.25
highest = lax.Precision.HIGHEST


def with_halo(shard, sides, width):
    for axis, dim in sides:
        peers, length = (lax.axis_size(axis), shard.shape[dim])
        up = [(i, (i + 1) % peers) for i in range(peers - 1)]
        down = [(j, i) for i, j in up]
        last = lax.slice_in_dim(shard, length - width, length, axis=dim)
        initial = lax.slice_in_dim(shard, 0, width, axis=dim)
        before = lax.ppermute(last, axis, up)
        after = lax.ppermute(initial, axis, down)
        shard = jnp.concatenate([before, shard, after], axis=dim)
    return shard


def spatial_pad(grid_field):
    return jnp.pad(grid_field, ((1, 1), (1, 1), (1, 1)))


def axial_pad(grid_field):
    return jnp.pad(grid_field, ((0, 0), (0, 0), (1, 1)))


def coefficients(cond_padded):
    centre = cond_padded[1:-1, 1:-1, 1:-1]
    face_terms = (
        0.5 * (centre + cond_padded[2:, 1:-1, 1:-1]),
        0.5 * (centre + cond_padded[:-2, 1:-1, 1:-1]),
        0.5 * (centre + cond_padded[1:-1, 2:, 1:-1]),
        0.5 * (centre + cond_padded[1:-1, :-2, 1:-1]),
        axial_ratio * 0.5 * (centre + cond_padded[1:-1, 1:-1, 2:]),
        axial_ratio * 0.5 * (centre + cond_padded[1:-1, 1:-1, :-2]),
    )
    diagonal = (
        face_terms[0]
        + face_terms[1]
        + face_terms[2]
        + face_terms[3]
        + face_terms[4]
        + face_terms[5]
    )
    return (face_terms, diagonal)


def apply_operator(face_terms, diagonal, padded):
    centre = padded[1:-1, 1:-1, 1:-1]
    beside = face_terms[0] * padded[2:, 1:-1, 1:-1] + face_terms[1] * padded[:-2, 1:-1, 1:-1]
    beside = (
        beside + face_terms[2] * padded[1:-1, 2:, 1:-1] + face_terms[3] * padded[1:-1, :-2, 1:-1]
    )
    beside = (
        beside + face_terms[4] * padded[1:-1, 1:-1, 2:] + face_terms[5] * padded[1:-1, 1:-1, :-2]
    )
    return diagonal * centre - beside


def margin(grid_field):
    return with_halo(grid_field, (("sx", 0), ("sy", 1)), MARGIN)


def faces_of(grid_field):
    return with_halo(grid_field, (("sx", 0), ("sy", 1)), 1)


def global_sums(partial_terms):
    return lax.psum(jnp.stack(partial_terms), ("sx", "sy"))


def sine_table(lines_count):
    positions = jnp.arange(lines_count, dtype=jnp.int32) + 1
    phase_index = positions[:, None] * positions[None, :] % (2 * (lines_count + 1))
    return jnp.sqrt(2.0 / (lines_count + 1)) * jnp.sin(
        jnp.pi * phase_index.astype(jnp.float32) / (lines_count + 1)
    )


def diffusion_gain(lines_count, cells_side):
    positions = (jnp.arange(lines_count, dtype=jnp.int32) + 1).astype(jnp.float32)
    half_sine = jnp.sin(0.5 * jnp.pi * positions / (lines_count + 1))
    stiffness = 8.0 * cells_side * cells_side * half_sine * half_sine
    return (1.0 - stiffness) / (1.0 + stiffness)


def per_device(right_side, class_map, conductivity_table, velocity):
    cells_x, cells_y, cells_z = right_side.shape
    picked = (class_map[..., None] == jnp.arange(CLASSES, dtype=jnp.int32)).astype(jnp.float32)
    block_values = jnp.sum(picked * conductivity_table, axis=-1)
    conductivity = jnp.repeat(jnp.repeat(jnp.repeat(block_values, 2, axis=0), 2, axis=1), 4, axis=2)
    cond_wide = margin(conductivity)
    local_faces, local_diagonal = coefficients(spatial_pad(cond_wide))
    inside = (cond_wide > 0.0).astype(jnp.float32)
    inverse = inside / (local_diagonal + (1.0 - inside))
    near_cells = cond_wide[MARGIN - 1 : MARGIN + cells_x + 1, MARGIN - 1 : MARGIN + cells_y + 1, :]
    own_faces, own_diagonal = coefficients(axial_pad(near_cells))

    def operate(padded_plane):
        return apply_operator(own_faces, own_diagonal, axial_pad(padded_plane))

    def precondition(residual):
        region = margin(residual)
        update = region * inverse
        for sweep_index in range(SWEEPS - 1):
            update = (
                update
                + (region - apply_operator(local_faces, local_diagonal, spatial_pad(update)))
                * inverse
            )
        return update[MARGIN : MARGIN + cells_x, MARGIN : MARGIN + cells_y, :]

    residual = right_side
    first_dir = precondition(residual)
    first_wide = faces_of(first_dir)
    image_one = operate(first_wide)
    totals = global_sums([jnp.sum(residual * image_one), jnp.sum(image_one * image_one)])
    weight_one = totals[1]
    alpha_one = totals[0] / weight_one
    residual = residual - alpha_one * image_one
    second_dir = precondition(residual)
    second_wide = faces_of(second_dir)
    image_two = operate(second_wide)
    beta_two = global_sums([jnp.sum(image_two * image_one)])[0] / weight_one
    image_two = image_two - beta_two * image_one
    totals = global_sums([jnp.sum(residual * image_two), jnp.sum(image_two * image_two)])
    alpha_two = totals[0] / totals[1]
    second_dir = second_dir - beta_two * first_dir
    potential = alpha_one * first_dir
    potential = potential + alpha_two * second_dir
    potential_wide = faces_of(potential)
    grad_x = 0.5 * (potential_wide[2:, 1:-1, :] - potential_wide[:-2, 1:-1, :])
    grad_y = 0.5 * (potential_wide[1:-1, 2:, :] - potential_wide[1:-1, :-2, :])
    lines_count = cells_y * lax.axis_size("sy")
    sine_rows = sine_table(lines_count)
    line_gain = diffusion_gain(lines_count, cells_y)[:, None]
    force_x = conductivity * (-grad_y - velocity[0])
    force_y = conductivity * (grad_x - velocity[1])
    moved_velocity = jnp.stack(
        [velocity[0] + coupling * force_x, velocity[1] + coupling * force_y, velocity[2]]
    )
    sine_coeffs = jnp.matmul(
        sine_rows,
        lax.all_to_all(moved_velocity, "sy", split_axis=1, concat_axis=2, tiled=True),
        precision=highest,
    )
    velocity_next = jnp.matmul(sine_rows, sine_coeffs * line_gain, precision=highest)
    return (potential, velocity_next)


def solution(mesh):
    return jax.shard_map(
        per_device,
        mesh=mesh,
        in_specs=(P("sx", "sy", None), P("sx", "sy", None), P(), P(None, "sx", "sy", None)),
        out_specs=(P("sx", "sy", None), P(None, ("sx", "sy"), None, None)),
        check_vma=False,
    )
```

profile of v0, /device:TPU:0, one launch (start us, length us, event | category | flops | bytes accessed | tf_op | source)
XLA Modules:
  0.0 262.0 jit_solution(9284805795825256897)
XLA Ops:
  0.6 1.1 select_reduce_fusion
  2.1 1.3 collective-permute-start
  3.6 5.6 %collective-permute-start.1 = (f32[4,16,128]{2,1,0:T(8,128)S(1)}, f32[4,16,128]{2,1,0:T(8,128)S(1)}, u32[]{:S(2)}, u32[]{:S(2)}) collective-permute-start(f32[4,16,128]{2,1,0:T(8,128)S(1)} %copy.246), channel_id=1, source_target_pairs={{0,8},{8,16},{16,24},{1,9},{9,17},{17,25},{2,10},{10,18},{18,26},{... | collective-permute-start | bytes 98312 | tf_op jit(solution)/shard_map/ppermute | solution.py:23
  9.2 3.9 %collective-permute-start.4 = (f32[4,16,128]{2,1,0:T(8,128)S(1)}, f32[4,16,128]{2,1,0:T(8,128)S(1)}, u32[]{:S(2)}, u32[]{:S(2)}) collective-permute-start(f32[4,16,128]{2,1,0:T(8,128)S(1)} %get-tuple-element.50), channel_id=1, source_target_pairs={{0,8},{8,16},{16,24},{1,9},{9,17},{17,25},{2,10},{10,18},{18,26},{... | collective-permute-start | bytes 98312 | tf_op jit(solution)/shard_map/ppermute | solution.py:23
  13.1 1.3 collective-permute-start.5
  14.8 0.5 copy.244
  15.3 1.3 collective-permute-start.2
  16.6 3.0 %collective-permute-start.3 = (f32[40,4,128]{2,1,0:T(4,128)S(1)}, f32[40,4,128]{2,1,0:T(4,128)S(1)}, u32[]{:S(2)}, u32[]{:S(2)}) collective-permute-start(f32[40,4,128]{2,1,0:T(4,128)S(1)} %get-tuple-element.35), channel_id=1, source_target_pairs={{0,1},{1,2},{2,3},{3,4},{4,5},{5,6},{6,7},{8,9},{9,10},{10,11},{11... | collective-permute-start | bytes 245768 | tf_op jit(solution)/shard_map/ppermute | solution.py:23
  19.8 3.0 %collective-permute-start.6 = (f32[40,4,128]{2,1,0:T(4,128)S(1)}, f32[40,4,128]{2,1,0:T(4,128)S(1)}, u32[]{:S(2)}, u32[]{:S(2)}) collective-permute-start(f32[40,4,128]{2,1,0:T(4,128)S(1)} %get-tuple-element.37), channel_id=1, source_target_pairs={{0,1},{1,2},{2,3},{3,4},{4,5},{5,6},{6,7},{8,9},{9,10},{10,11},{11... | collective-permute-start | bytes 245768 | tf_op jit(solution)/shard_map/ppermute | solution.py:23
  22.8 1.3 collective-permute-start.7
  24.3 1.7 collective-permute-done.7
  26.0 1.6 fusion.212
  27.6 0.6 fusion.24
  28.2 0.6 fusion.39
  28.8 0.6 fusion.54
  29.4 0.6 fusion.69
  30.0 1.3 collective-permute-start.8
  31.3 5.2 %collective-permute-start.9 = (f32[1,16,128]{2,1,0:T(8,128)S(1)}, f32[1,16,128]{2,1,0:T(8,128)S(1)}, u32[]{:S(2)}, u32[]{:S(2)}) collective-permute-start(f32[1,16,128]{2,1,0:T(8,128)S(1)} %get-tuple-element.31), channel_id=1, source_target_pairs={{0,8},{8,16},{16,24},{1,9},{9,17},{17,25},{2,10},{10,18},{18,26},{... | collective-permute-start | bytes 24584 | tf_op jit(solution)/shard_map/ppermute | solution.py:23
  36.5 1.3 collective-permute-done.9
  37.9 1.4 collective-permute-start.10
  39.3 4.8 %collective-permute-start.11 = (f32[34,1,128]{2,1,0:T(1,128)S(1)}, f32[34,1,128]{2,1,0:T(1,128)S(1)}, u32[]{:S(2)}, u32[]{:S(2)}) collective-permute-start(f32[34,1,128]{2,1,0:T(1,128)S(1)} %get-tuple-element.43), channel_id=1, source_target_pairs={{0,1},{1,2},{2,3},{3,4},{4,5},{5,6},{6,7},{8,9},{9,10},{10,11},{11... | collective-permute-start | bytes 52232 | tf_op jit(solution)/shard_map/ppermute | solution.py:23
  44.1 0.8 collective-permute-done.11
  44.9 0.4 select_maximum_fusion.4
  45.4 1.9 multiply_reduce_fusion.4
  47.3 2.0 pad_maximum_fusion.51
  49.3 45.0 %psum.21 = f32[2]{0:T(128)} all-reduce(f32[2]{0:T(128)} %pad_maximum_fusion.51), channel_id=1, replica_groups=mesh['sx'=4,'sy'=8] {'sx','sy'}, use_global_device_ids=true, to_apply=%region_3.4 | all-reduce | flops 2 | bytes 16 | tf_op jit(solution)/shard_map/psum | solution.py:79
  94.3 1.4 fusion.230
  97.1 1.1 multiply_subtract_fusion.1
  98.1 3.4 %collective-permute-start.12 = (f32[4,16,128]{2,1,0:T(8,128)S(1)}, f32[4,16,128]{2,1,0:T(8,128)S(1)}, u32[]{:S(2)}, u32[]{:S(2)}) collective-permute-start(f32[4,16,128]{2,1,0:T(8,128)S(1)} %get-tuple-element.47), channel_id=1, source_target_pairs={{0,8},{8,16},{16,24},{1,9},{9,17},{17,25},{2,10},{10,18},{18,26},{... | collective-permute-start | bytes 98312 | tf_op jit(solution)/shard_map/ppermute | solution.py:23
  101.6 1.3 collective-permute-start.13
  102.9 0.3 collective-permute-done.12
  103.1 4.2 %collective-permute-done.13 = f32[4,16,128]{2,1,0:T(8,128)S(1)} collective-permute-done((f32[4,16,128]{2,1,0:T(8,128)S(1)}, f32[4,16,128]{2,1,0:T(8,128)S(1)}, u32[]{:S(2)}, u32[]{:S(2)}) %collective-permute-start.13) | collective-permute-done | bytes 32800 | tf_op jit(solution)/shard_map/ppermute | solution.py:24
  107.4 1.3 collective-permute-start.14
  108.7 1.3 collective-permute-start.15
  110.0 4.4 %collective-permute-done.15 = f32[40,4,128]{2,1,0:T(4,128)S(1)} collective-permute-done((f32[40,4,128]{2,1,0:T(4,128)S(1)}, f32[40,4,128]{2,1,0:T(4,128)S(1)}, u32[]{:S(2)}, u32[]{:S(2)}) %collective-permute-start.15) | collective-permute-done | bytes 81952 | tf_op jit(solution)/shard_map/ppermute | solution.py:24
  114.5 0.5 fusion.84
  115.0 0.5 fusion.99
  115.6 0.5 fusion.114
  116.1 0.5 fusion.129
  116.7 1.4 collective-permute-start.16
  118.2 4.5 %collective-permute-start.17 = (f32[1,16,128]{2,1,0:T(8,128)S(1)}, f32[1,16,128]{2,1,0:T(8,128)S(1)}, u32[]{:S(2)}, u32[]{:S(2)}) collective-permute-start(f32[1,16,128]{2,1,0:T(8,128)S(1)} %get-tuple-element.29), channel_id=1, source_target_pairs={{0,8},{8,16},{16,24},{1,9},{9,17},{17,25},{2,10},{10,18},{18,26},{... | collective-permute-start | bytes 24584 | tf_op jit(solution)/shard_map/ppermute | solution.py:23
  122.8 1.3 collective-permute-done.17
  124.1 1.3 collective-permute-start.18
  125.4 4.5 %collective-permute-start.19 = (f32[34,1,128]{2,1,0:T(1,128)S(1)}, f32[34,1,128]{2,1,0:T(1,128)S(1)}, u32[]{:S(2)}, u32[]{:S(2)}) collective-permute-start(f32[34,1,128]{2,1,0:T(1,128)S(1)} %get-tuple-element.41), channel_id=1, source_target_pairs={{0,1},{1,2},{2,3},{3,4},{4,5},{5,6},{6,7},{8,9},{9,10},{10,11},{11... | collective-permute-start | bytes 52232 | tf_op jit(solution)/shard_map/ppermute | solution.py:23
  129.9 0.8 collective-permute-done.19
  130.7 0.4 select_maximum_fusion
  131.2 1.1 multiply_reduce_fusion.2
  132.4 45.0 %psum.22 = f32[1]{0:T(128)} all-reduce(f32[1]{0:T(128)} %bitcast.12), channel_id=1, replica_groups=mesh['sx'=4,'sy'=8] {'sx','sy'}, use_global_device_ids=true, to_apply=%region_5.6 | all-reduce | flops 1 | bytes 8 | tf_op jit(solution)/shard_map/psum | solution.py:79
  178.7 0.8 multiply_reduce_fusion.1
  179.5 1.3 pad_maximum_fusion.52
  180.8 40.5 %psum.23 = f32[2]{0:T(128)S(1)} all-reduce(f32[2]{0:T(128)S(1)} %pad_maximum_fusion.52), channel_id=1, replica_groups=mesh['sx'=4,'sy'=8] {'sx','sy'}, use_global_device_ids=true, to_apply=%region_8.9 | all-reduce | flops 2 | bytes 16 | tf_op jit(solution)/shard_map/psum | solution.py:79
  221.3 0.6 fusion.229
  223.2 1.1 multiply_add_fusion
  224.3 3.5 %collective-permute-start.20 = (f32[1,16,128]{2,1,0:T(8,128)S(1)}, f32[1,16,128]{2,1,0:T(8,128)S(1)}, u32[]{:S(2)}, u32[]{:S(2)}) collective-permute-start(f32[1,16,128]{2,1,0:T(8,128)S(1)} %get-tuple-element.46), channel_id=1, source_target_pairs={{0,8},{8,16},{16,24},{1,9},{9,17},{17,25},{2,10},{10,18},{18,26},{... | collective-permute-start | bytes 24584 | tf_op jit(solution)/shard_map/ppermute | solution.py:23
  227.9 1.3 collective-permute-start.21
  229.2 4.2 %collective-permute-done.21 = f32[1,16,128]{2,1,0:T(8,128)S(1)} collective-permute-done((f32[1,16,128]{2,1,0:T(8,128)S(1)}, f32[1,16,128]{2,1,0:T(8,128)S(1)}, u32[]{:S(2)}, u32[]{:S(2)}) %collective-permute-start.21) | collective-permute-done | bytes 8224 | tf_op jit(solution)/shard_map/ppermute | solution.py:24
  233.4 1.3 collective-permute-start.22
  234.7 3.2 %collective-permute-start.23 = (f32[34,1,128]{2,1,0:T(1,128)S(1)}, f32[34,1,128]{2,1,0:T(1,128)S(1)}, u32[]{:S(2)}, u32[]{:S(2)}) collective-permute-start(f32[34,1,128]{2,1,0:T(1,128)S(1)} %get-tuple-element.40), channel_id=1, source_target_pairs={{0,1},{1,2},{2,3},{3,4},{4,5},{5,6},{6,7},{8,9},{9,10},{10,11},{11... | collective-permute-start | bytes 52232 | tf_op jit(solution)/shard_map/ppermute | solution.py:23
  237.9 0.8 collective-permute-done.23
  239.0 0.9 copy.256
  239.9 6.3 %all-to-all-start = ((f32[3,32,16,128]{3,2,0,1:T(8,128)}), f32[3,32,16,128]{3,2,0,1:T(8,128)S(1)}, u32[]{:S(2)}, u32[]{:S(2)}) async-start(f32[3,32,16,128]{3,2,0,1:T(8,128)} %copy.256), calls=%async_computation | async-start | bytes 1572864 | tf_op jit(solution)/shard_map/all_to_all | solution.py:154
  246.3 12.5 %all-to-all-done = f32[3,32,16,128]{3,2,0,1:T(8,128)S(1)} async-done(((f32[3,32,16,128]{3,2,0,1:T(8,128)}), f32[3,32,16,128]{3,2,0,1:T(8,128)S(1)}, u32[]{:S(2)}, u32[]{:S(2)}) %all-to-all-start) | async-done | bytes 786464 | tf_op jit(solution)/shard_map/all_to_all | solution.py:154
  258.9 1.1 fusion
  260.0 2.0 convolution_bitcast_fusion
  (95 shorter events, 1.8 us)
Async XLA Ops:
  0.6 8.6 %copy-start.8 = (f32[32,16,128]{2,1,0:T(8,128)S(1)}, f32[32,16,128]{2,1,0:T(8,128)}, u32[]{:S(2)}) copy-start(f32[32,16,128]{2,1,0:T(8,128)} %param.4) | copy-start | bytes 786436
  2.1 13.2 %collective-permute-start = (f32[4,16,128]{2,1,0:T(8,128)S(1)}, f32[4,16,128]{2,1,0:T(8,128)S(1)}, u32[]{:S(2)}, u32[]{:S(2)}) collective-permute-start(f32[4,16,128]{2,1,0:T(8,128)S(1)} %copy.242), channel_id=1, source_target_pairs={{8,0},{16,8},{24,16},{9,1},{17,9},{25,17},{10,2},{18,10},{26,18},{... | collective-permute-start | bytes 98312 | tf_op jit(solution)/shard_map/ppermute | solution.py:24
  3.6 11.7 %collective-permute-start.1 = (f32[4,16,128]{2,1,0:T(8,128)S(1)}, f32[4,16,128]{2,1,0:T(8,128)S(1)}, u32[]{:S(2)}, u32[]{:S(2)}) collective-permute-start(f32[4,16,128]{2,1,0:T(8,128)S(1)} %copy.246), channel_id=1, source_target_pairs={{0,8},{8,16},{16,24},{1,9},{9,17},{17,25},{2,10},{10,18},{18,26},{... | collective-permute-start | bytes 98312 | tf_op jit(solution)/shard_map/ppermute | solution.py:23
  9.2 10.5 %collective-permute-start.4 = (f32[4,16,128]{2,1,0:T(8,128)S(1)}, f32[4,16,128]{2,1,0:T(8,128)S(1)}, u32[]{:S(2)}, u32[]{:S(2)}) collective-permute-start(f32[4,16,128]{2,1,0:T(8,128)S(1)} %get-tuple-element.50), channel_id=1, source_target_pairs={{0,8},{8,16},{16,24},{1,9},{9,17},{17,25},{2,10},{10,18},{18,26},{... | collective-permute-start | bytes 98312 | tf_op jit(solution)/shard_map/ppermute | solution.py:23
  13.1 6.6 %collective-permute-start.5 = (f32[4,16,128]{2,1,0:T(8,128)S(1)}, f32[4,16,128]{2,1,0:T(8,128)S(1)}, u32[]{:S(2)}, u32[]{:S(2)}) collective-permute-start(f32[4,16,128]{2,1,0:T(8,128)S(1)} %get-tuple-element.49), channel_id=1, source_target_pairs={{8,0},{16,8},{24,16},{9,1},{17,9},{25,17},{10,2},{18,10},{26,18},{... | collective-permute-start | bytes 98312 | tf_op jit(solution)/shard_map/ppermute | solution.py:24
  15.3 9.0 %copy-start.2 = (f32[32,16,128]{2,1,0:T(8,128)}, f32[32,16,128]{2,1,0:T(8,128)S(1)}, u32[]{:S(2)}) copy-start(f32[32,16,128]{2,1,0:T(8,128)S(1)} %copy.244) | copy-start | bytes 786436
  15.3 9.0 %copy-start.17 = (f32[4,16,128]{2,1,0:T(8,128)}, f32[4,16,128]{2,1,0:T(8,128)S(1)}, u32[]{:S(2)}) copy-start(f32[4,16,128]{2,1,0:T(8,128)S(1)} %collective-permute-done.1) | copy-start | bytes 98308
  15.3 8.8 %collective-permute-start.2 = (f32[40,4,128]{2,1,0:T(4,128)S(1)}, f32[40,4,128]{2,1,0:T(4,128)S(1)}, u32[]{:S(2)}, u32[]{:S(2)}) collective-permute-start(f32[40,4,128]{2,1,0:T(4,128)S(1)} %get-tuple-element.36), channel_id=1, source_target_pairs={{1,0},{2,1},{3,2},{4,3},{5,4},{6,5},{7,6},{9,8},{10,9},{11,10},{12... | collective-permute-start | bytes 245768 | tf_op jit(solution)/shard_map/ppermute | solution.py:24
  16.6 7.5 %collective-permute-start.3 = (f32[40,4,128]{2,1,0:T(4,128)S(1)}, f32[40,4,128]{2,1,0:T(4,128)S(1)}, u32[]{:S(2)}, u32[]{:S(2)}) collective-permute-start(f32[40,4,128]{2,1,0:T(4,128)S(1)} %get-tuple-element.35), channel_id=1, source_target_pairs={{0,1},{1,2},{2,3},{3,4},{4,5},{5,6},{6,7},{8,9},{9,10},{10,11},{11... | collective-permute-start | bytes 245768 | tf_op jit(solution)/shard_map/ppermute | solution.py:23
  19.8 4.5 %collective-permute-start.6 = (f32[40,4,128]{2,1,0:T(4,128)S(1)}, f32[40,4,128]{2,1,0:T(4,128)S(1)}, u32[]{:S(2)}, u32[]{:S(2)}) collective-permute-start(f32[40,4,128]{2,1,0:T(4,128)S(1)} %get-tuple-element.37), channel_id=1, source_target_pairs={{0,1},{1,2},{2,3},{3,4},{4,5},{5,6},{6,7},{8,9},{9,10},{10,11},{11... | collective-permute-start | bytes 245768 | tf_op jit(solution)/shard_map/ppermute | solution.py:23
  22.8 3.2 %collective-permute-start.7 = (f32[40,4,128]{2,1,0:T(4,128)S(1)}, f32[40,4,128]{2,1,0:T(4,128)S(1)}, u32[]{:S(2)}, u32[]{:S(2)}) collective-permute-start(f32[40,4,128]{2,1,0:T(4,128)S(1)} %get-tuple-element.38), channel_id=1, source_target_pairs={{1,0},{2,1},{3,2},{4,3},{5,4},{6,5},{7,6},{9,8},{10,9},{11,10},{12... | collective-permute-start | bytes 245768 | tf_op jit(solution)/shard_map/ppermute | solution.py:24
  24.1 21.2 %copy-start.14 = (f32[40,4,128]{2,1,0:T(4,128)}, f32[40,4,128]{2,1,0:T(4,128)S(1)}, u32[]{:S(2)}) copy-start(f32[40,4,128]{2,1,0:T(4,128)S(1)} %collective-permute-done.3) | copy-start | bytes 245764
  29.9 15.4 %copy-start.11 = (f32[40,24,128]{2,1,0:T(8,128)}, f32[40,24,128]{2,1,0:T(8,128)S(1)}, u32[]{:S(2)}) copy-start(f32[40,24,128]{2,1,0:T(8,128)S(1)} %fusion.69) | copy-start | bytes 1474564
  30.0 6.5 %collective-permute-start.8 = (f32[1,16,128]{2,1,0:T(8,128)S(1)}, f32[1,16,128]{2,1,0:T(8,128)S(1)}, u32[]{:S(2)}, u32[]{:S(2)}) collective-permute-start(f32[1,16,128]{2,1,0:T(8,128)S(1)} %get-tuple-element.32), channel_id=1, source_target_pairs={{8,0},{16,8},{24,16},{9,1},{17,9},{25,17},{10,2},{18,10},{26,18},{... | collective-permute-start | bytes 24584 | tf_op jit(solution)/shard_map/ppermute | solution.py:24
  31.3 6.5 %collective-permute-start.9 = (f32[1,16,128]{2,1,0:T(8,128)S(1)}, f32[1,16,128]{2,1,0:T(8,128)S(1)}, u32[]{:S(2)}, u32[]{:S(2)}) collective-permute-start(f32[1,16,128]{2,1,0:T(8,128)S(1)} %get-tuple-element.31), channel_id=1, source_target_pairs={{0,8},{8,16},{16,24},{1,9},{9,17},{17,25},{2,10},{10,18},{18,26},{... | collective-permute-start | bytes 24584 | tf_op jit(solution)/shard_map/ppermute | solution.py:23
  37.8 7.5 %copy-start.3 = (f32[32,16,128]{2,1,0:T(8,128)S(1)}, f32[32,16,128]{2,1,0:T(8,128)}, u32[]{:S(2)}) copy-start(f32[32,16,128]{2,1,0:T(8,128)} %copy-done.2) | copy-start | bytes 786436
  37.8 7.5 %copy-start.9 = (f32[32,16,128]{2,1,0:T(8,128)S(1)}, f32[32,16,128]{2,1,0:T(8,128)}, u32[]{:S(2)}) copy-start(f32[32,16,128]{2,1,0:T(8,128)} %param.4) | copy-start | bytes 786436
  37.9 7.5 %copy-start.18 = (f32[4,16,128]{2,1,0:T(8,128)S(1)}, f32[4,16,128]{2,1,0:T(8,128)}, u32[]{:S(2)}) copy-start(f32[4,16,128]{2,1,0:T(8,128)} %copy-done.17) | copy-start | bytes 98308
  37.9 6.3 %collective-permute-start.10 = (f32[34,1,128]{2,1,0:T(1,128)S(1)}, f32[34,1,128]{2,1,0:T(1,128)S(1)}, u32[]{:S(2)}, u32[]{:S(2)}) collective-permute-start(f32[34,1,128]{2,1,0:T(1,128)S(1)} %get-tuple-element.44), channel_id=1, source_target_pairs={{1,0},{2,1},{3,2},{4,3},{5,4},{6,5},{7,6},{9,8},{10,9},{11,10},{12... | collective-permute-start | bytes 52232 | tf_op jit(solution)/shard_map/ppermute | solution.py:24
  39.3 5.6 %collective-permute-start.11 = (f32[34,1,128]{2,1,0:T(1,128)S(1)}, f32[34,1,128]{2,1,0:T(1,128)S(1)}, u32[]{:S(2)}, u32[]{:S(2)}) collective-permute-start(f32[34,1,128]{2,1,0:T(1,128)S(1)} %get-tuple-element.43), channel_id=1, source_target_pairs={{0,1},{1,2},{2,3},{3,4},{4,5},{5,6},{6,7},{8,9},{9,10},{10,11},{11... | collective-permute-start | bytes 52232 | tf_op jit(solution)/shard_map/ppermute | solution.py:23
  44.1 3.2 %copy-start.6 = (f32[34,18,128]{2,1,0:T(8,128)}, f32[34,18,128]{2,1,0:T(8,128)S(1)}, u32[]{:S(2)}) copy-start(f32[34,18,128]{2,1,0:T(8,128)S(1)} %slice.535) | copy-start | bytes 940036
  98.1 18.0 %copy-start = (f32[32,16,128]{2,1,0:T(8,128)}, f32[32,16,128]{2,1,0:T(8,128)S(1)}, u32[]{:S(2)}) copy-start(f32[32,16,128]{2,1,0:T(8,128)S(1)} %multiply_subtract_fusion.1) | copy-start | bytes 786436
  98.1 5.0 %collective-permute-start.12 = (f32[4,16,128]{2,1,0:T(8,128)S(1)}, f32[4,16,128]{2,1,0:T(8,128)S(1)}, u32[]{:S(2)}, u32[]{:S(2)}) collective-permute-start(f32[4,16,128]{2,1,0:T(8,128)S(1)} %get-tuple-element.47), channel_id=1, source_target_pairs={{0,8},{8,16},{16,24},{1,9},{9,17},{17,25},{2,10},{10,18},{18,26},{... | collective-permute-start | bytes 98312 | tf_op jit(solution)/shard_map/ppermute | solution.py:23
  101.6 5.8 %collective-permute-start.13 = (f32[4,16,128]{2,1,0:T(8,128)S(1)}, f32[4,16,128]{2,1,0:T(8,128)S(1)}, u32[]{:S(2)}, u32[]{:S(2)}) collective-permute-start(f32[4,16,128]{2,1,0:T(8,128)S(1)} %get-tuple-element.48), channel_id=1, source_target_pairs={{8,0},{16,8},{24,16},{9,1},{17,9},{25,17},{10,2},{18,10},{26,18},{... | collective-permute-start | bytes 98312 | tf_op jit(solution)/shard_map/ppermute | solution.py:24
  107.4 2.6 collective-permute-start.14
  108.7 5.7 %collective-permute-start.15 = (f32[40,4,128]{2,1,0:T(4,128)S(1)}, f32[40,4,128]{2,1,0:T(4,128)S(1)}, u32[]{:S(2)}, u32[]{:S(2)}) collective-permute-start(f32[40,4,128]{2,1,0:T(4,128)S(1)} %get-tuple-element.34), channel_id=1, source_target_pairs={{1,0},{2,1},{3,2},{4,3},{5,4},{6,5},{7,6},{9,8},{10,9},{11,10},{12... | collective-permute-start | bytes 245768 | tf_op jit(solution)/shard_map/ppermute | solution.py:24
  116.7 15.7 %copy-start.13 = (f32[40,24,128]{2,1,0:T(8,128)}, f32[40,24,128]{2,1,0:T(8,128)S(1)}, u32[]{:S(2)}) copy-start(f32[40,24,128]{2,1,0:T(8,128)S(1)} %fusion.129) | copy-start | bytes 1474564
  116.7 14.5 %copy-start.4 = (f32[32,16,128]{2,1,0:T(8,128)S(1)}, f32[32,16,128]{2,1,0:T(8,128)}, u32[]{:S(2)}) copy-start(f32[32,16,128]{2,1,0:T(8,128)} %copy-done.2) | copy-start | bytes 786436
  116.7 14.5 %copy-start.5 = (f32[32,16,128]{2,1,0:T(8,128)S(1)}, f32[32,16,128]{2,1,0:T(8,128)}, u32[]{:S(2)}) copy-start(f32[32,16,128]{2,1,0:T(8,128)} %get-tuple-element.18) | copy-start | bytes 786436
  116.7 14.5 %copy-start.7 = (f32[34,18,128]{2,1,0:T(8,128)S(1)}, f32[34,18,128]{2,1,0:T(8,128)}, u32[]{:S(2)}) copy-start(f32[34,18,128]{2,1,0:T(8,128)} %copy-done.6) | copy-start | bytes 940036
  116.7 14.5 %copy-start.15 = (f32[40,4,128]{2,1,0:T(4,128)S(1)}, f32[40,4,128]{2,1,0:T(4,128)}, u32[]{:S(2)}) copy-start(f32[40,4,128]{2,1,0:T(4,128)} %copy-done.14) | copy-start | bytes 245764
  116.7 14.5 %copy-start.19 = (f32[4,16,128]{2,1,0:T(8,128)S(1)}, f32[4,16,128]{2,1,0:T(8,128)}, u32[]{:S(2)}) copy-start(f32[4,16,128]{2,1,0:T(8,128)} %copy-done.17) | copy-start | bytes 98308
  116.7 6.0 %collective-permute-start.16 = (f32[1,16,128]{2,1,0:T(8,128)S(1)}, f32[1,16,128]{2,1,0:T(8,128)S(1)}, u32[]{:S(2)}, u32[]{:S(2)}) collective-permute-start(f32[1,16,128]{2,1,0:T(8,128)S(1)} %get-tuple-element.30), channel_id=1, source_target_pairs={{8,0},{16,8},{24,16},{9,1},{17,9},{25,17},{10,2},{18,10},{26,18},{... | collective-permute-start | bytes 24584 | tf_op jit(solution)/shard_map/ppermute | solution.py:24
  118.2 5.9 %collective-permute-start.17 = (f32[1,16,128]{2,1,0:T(8,128)S(1)}, f32[1,16,128]{2,1,0:T(8,128)S(1)}, u32[]{:S(2)}, u32[]{:S(2)}) collective-permute-start(f32[1,16,128]{2,1,0:T(8,128)S(1)} %get-tuple-element.29), channel_id=1, source_target_pairs={{0,8},{8,16},{16,24},{1,9},{9,17},{17,25},{2,10},{10,18},{18,26},{... | collective-permute-start | bytes 24584 | tf_op jit(solution)/shard_map/ppermute | solution.py:23
  124.1 5.8 %collective-permute-start.18 = (f32[34,1,128]{2,1,0:T(1,128)S(1)}, f32[34,1,128]{2,1,0:T(1,128)S(1)}, u32[]{:S(2)}, u32[]{:S(2)}) collective-permute-start(f32[34,1,128]{2,1,0:T(1,128)S(1)} %get-tuple-element.42), channel_id=1, source_target_pairs={{1,0},{2,1},{3,2},{4,3},{5,4},{6,5},{7,6},{9,8},{10,9},{11,10},{12... | collective-permute-start | bytes 52232 | tf_op jit(solution)/shard_map/ppermute | solution.py:24
  125.4 5.3 %collective-permute-start.19 = (f32[34,1,128]{2,1,0:T(1,128)S(1)}, f32[34,1,128]{2,1,0:T(1,128)S(1)}, u32[]{:S(2)}, u32[]{:S(2)}) collective-permute-start(f32[34,1,128]{2,1,0:T(1,128)S(1)} %get-tuple-element.41), channel_id=1, source_target_pairs={{0,1},{1,2},{2,3},{3,4},{4,5},{5,6},{6,7},{8,9},{9,10},{10,11},{11... | collective-permute-start | bytes 52232 | tf_op jit(solution)/shard_map/ppermute | solution.py:23
  131.2 47.5 %copy-start.1 = (f32[32,16,128]{2,1,0:T(8,128)S(1)}, f32[32,16,128]{2,1,0:T(8,128)}, u32[]{:S(2)}) copy-start(f32[32,16,128]{2,1,0:T(8,128)} %copy-done) | copy-start | bytes 786436
  131.2 92.0 %copy-start.12 = (f32[40,24,128]{2,1,0:T(8,128)S(1)}, f32[40,24,128]{2,1,0:T(8,128)}, u32[]{:S(2)}) copy-start(f32[40,24,128]{2,1,0:T(8,128)} %copy-done.11) | copy-start | bytes 1474564
  178.7 60.0 %copy-start.16 = (f32[3,32,16,128]{3,2,1,0:T(8,128)S(1)}, f32[3,32,16,128]{3,2,1,0:T(8,128)}, u32[]{:S(2)}) copy-start(f32[3,32,16,128]{3,2,1,0:T(8,128)} %param.7) | copy-start | bytes 2359300
  224.3 14.6 %copy-start.10 = (f32[32,16,128]{2,1,0:T(8,128)}, f32[32,16,128]{2,1,0:T(8,128)S(1)}, u32[]{:S(2)}) copy-start(f32[32,16,128]{2,1,0:T(8,128)S(1)} %multiply_add_fusion) | copy-start | bytes 786436
  224.3 4.9 %collective-permute-start.20 = (f32[1,16,128]{2,1,0:T(8,128)S(1)}, f32[1,16,128]{2,1,0:T(8,128)S(1)}, u32[]{:S(2)}, u32[]{:S(2)}) collective-permute-start(f32[1,16,128]{2,1,0:T(8,128)S(1)} %get-tuple-element.46), channel_id=1, source_target_pairs={{0,8},{8,16},{16,24},{1,9},{9,17},{17,25},{2,10},{10,18},{18,26},{... | collective-permute-start | bytes 24584 | tf_op jit(solution)/shard_map/ppermute | solution.py:23
  227.9 5.5 %collective-permute-start.21 = (f32[1,16,128]{2,1,0:T(8,128)S(1)}, f32[1,16,128]{2,1,0:T(8,128)S(1)}, u32[]{:S(2)}, u32[]{:S(2)}) collective-permute-start(f32[1,16,128]{2,1,0:T(8,128)S(1)} %get-tuple-element.45), channel_id=1, source_target_pairs={{8,0},{16,8},{24,16},{9,1},{17,9},{25,17},{10,2},{18,10},{26,18},{... | collective-permute-start | bytes 24584 | tf_op jit(solution)/shard_map/ppermute | solution.py:24
  233.4 4.5 %collective-permute-start.22 = (f32[34,1,128]{2,1,0:T(1,128)S(1)}, f32[34,1,128]{2,1,0:T(1,128)S(1)}, u32[]{:S(2)}, u32[]{:S(2)}) collective-permute-start(f32[34,1,128]{2,1,0:T(1,128)S(1)} %get-tuple-element.39), channel_id=1, source_target_pairs={{1,0},{2,1},{3,2},{4,3},{5,4},{6,5},{7,6},{9,8},{10,9},{11,10},{12... | collective-permute-start | bytes 52232 | tf_op jit(solution)/shard_map/ppermute | solution.py:24
  234.7 4.2 %slice-start = ((f32[3,32,16,128]{3,2,1,0:T(8,128)}), f32[1,32,16,128]{3,2,1,0:T(8,128)S(1)}, s32[]{:S(2)}) async-start(f32[3,32,16,128]{3,2,1,0:T(8,128)} %param.7), calls=%async_computation.1 | async-start | bytes 524288 | tf_op jit(solution)/shard_map/slice | solution.py:150
  234.7 4.0 %collective-permute-start.23 = (f32[34,1,128]{2,1,0:T(1,128)S(1)}, f32[34,1,128]{2,1,0:T(1,128)S(1)}, u32[]{:S(2)}, u32[]{:S(2)}) collective-permute-start(f32[34,1,128]{2,1,0:T(1,128)S(1)} %get-tuple-element.40), channel_id=1, source_target_pairs={{0,1},{1,2},{2,3},{3,4},{4,5},{5,6},{6,7},{8,9},{9,10},{10,11},{11... | collective-permute-start | bytes 52232 | tf_op jit(solution)/shard_map/ppermute | solution.py:23
  239.9 18.9 %all-to-all-start = ((f32[3,32,16,128]{3,2,0,1:T(8,128)}), f32[3,32,16,128]{3,2,0,1:T(8,128)S(1)}, u32[]{:S(2)}, u32[]{:S(2)}) async-start(f32[3,32,16,128]{3,2,0,1:T(8,128)} %copy.256), calls=%async_computation | async-start | bytes 1572864 | tf_op jit(solution)/shard_map/all_to_all | solution.py:154
where the time goes:
time: 263 us; the launch traced here: 262 us
  blocking collectives  131 us (50%)
  starting transfers between devices  67.9 us (26%)
  waiting for transfers between devices  32.4 us (12%)
  other arithmetic  17.9 us (7%)
  between operations  5.52 us (2%)
  local copies, waits for them, and re-layouts  4.56 us (2%)
  matrix products  3.08 us (1%)
    psum x3, blocking collectives, global_sums(): return lax.psum(jnp.stack(partial_terms), ('sx', 'sy'))  131 us
    ppermute x12, starting transfers between devices, with_halo(): before = lax.ppermute(last, axis, up)  45.9 us
    ppermute x12, starting transfers between devices, with_halo(): after = lax.ppermute(initial, axis, down)  15.8 us
    ppermute x12, waiting for transfers between devices, with_halo(): after = lax.ppermute(initial, axis, down)  14.5 us
    all_to_all x1, waiting for transfers between devices, per_device(): lax.all_to_all(moved_velocity, 'sy', split_axis=1, concat_axis=2, tiled=T...  12.5 us
    all_to_all x1, starting transfers between devices, per_device(): lax.all_to_all(moved_velocity, 'sy', split_axis=1, concat_axis=2, tiled=T...  6.28 us
    ppermute x12, waiting for transfers between devices, with_halo(): before = lax.ppermute(last, axis, up)  5.33 us
  transfers between devices with their start and end apart: 25, of which 11 were waited for; matrix products, arithmetic and copies ran while one was open for 1% of the time, Pallas kernels for 0%

commit v1 on v0

v1 whole, which is shorter than its diff:
```python
import functools

import jax
import jax.numpy as jnp
import numpy as np
from jax import lax
from jax.experimental import pallas as pl
from jax.experimental.pallas import tpu as pltpu
from jax.sharding import PartitionSpec as P

MARGIN = 4
SWEEPS = 5
CLASSES = 8

axial_ratio = 0.0625
coupling = 0.25
highest = lax.Precision.HIGHEST
MESH = pl.DeviceIdType.MESH
DIAGONALS = ((-1, -1), (-1, 1), (1, -1), (1, 1))


def line_matrix(lines_count, cells_side):
    positions = np.arange(lines_count, dtype=np.int64) + 1
    phase = (positions[:, None] * positions[None, :]) % (2 * (lines_count + 1))
    sines = np.sqrt(2.0 / (lines_count + 1)) * np.sin(np.pi * phase / (lines_count + 1))
    half = np.sin(0.5 * np.pi * positions / (lines_count + 1))
    stiff = 8.0 * cells_side * cells_side * half * half
    gain = (1.0 - stiff) / (1.0 + stiff)
    return ((sines * gain[None, :]) @ sines).astype(np.float32)


def kernel(
    n_sx, n_sy, right_ref, class_ref, table_ref, velocity_ref, matrix_ref,
    potential_ref, next_ref,
    blk, blk_y, blk_c, got_bx, got_by, got_bc, wide_blk, cond,
    res_y, res_c, got_rx, got_ry, got_rc,
    img_y, img_c, got_ix, got_iy, got_ic,
    first_y, got_fx, got_fy, q_y, got_qx, got_qy,
    region, start, buf_a, buf_b, buf_q,
    bxp, bxm, byp, bym, bzp, bzm, inv, diag,
    first_own, image, q_own,
    line_v, line_c, line_f, line_q, sums_mine, sums_x, sums_row, sums_y,
    halo_send, halo_recv, face_send, face_recv, a2a_send, a2a_recv, local_sem,
    sx_send, sx_recv, sy_send, sy_recv,
):
    p, q = lax.axis_index("sx"), lax.axis_index("sy")
    cx, cy, nz = right_ref.shape
    hx, hy = cx // 2, cy // 2
    m = cx // n_sy
    mb = max(1, m // 2)
    ex, ey = cx + 2 * MARGIN, cy + 2 * MARGIN
    M = MARGIN
    H = M // 2
    lines_count = cy * n_sy

    def exists(dx, dy):
        ok = None
        for at, d, n in ((p, dx, n_sx), (q, dy, n_sy)):
            if d:
                this = (at + d >= 0) & (at + d < n)
                ok = this if ok is None else ok & this
        return ok

    barrier = pltpu.get_barrier_semaphore()

    def greet_y(k, _):
        pl.semaphore_signal(barrier, inc=1, device_id=(p, lax.rem(q + k, n_sy)), device_id_type=MESH)
        return 0

    def greet_x(k, _):
        pl.semaphore_signal(barrier, inc=1, device_id=(lax.rem(p + k, n_sx), q), device_id_type=MESH)
        return 0

    lax.fori_loop(1, n_sy, greet_y, 0)
    lax.fori_loop(1, n_sx, greet_x, 0)
    for dx, dy in DIAGONALS:
        @pl.when(exists(dx, dy))
        def _(dx=dx, dy=dy):
            pl.semaphore_signal(barrier, inc=1, device_id=(p + dx, q + dy), device_id_type=MESH)

    classes = class_ref[...].reshape(hx * hy, class_ref.shape[2])
    picked = jnp.zeros(classes.shape, jnp.float32)
    for one in range(CLASSES):
        picked = jnp.where(classes == one, table_ref[one], picked)
    zb = classes.shape[1]
    per = nz // zb
    wide = lax.broadcasted_iota(jnp.int32, (zb, nz), 1) - per * lax.broadcasted_iota(jnp.int32, (zb, nz), 0)
    spread = jnp.where((wide >= 0) & (wide < per), 1.0, 0.0).astype(jnp.float32)
    blk[...] = jnp.dot(picked, spread, precision=highest, preferred_element_type=jnp.float32).reshape(hx, hy, nz)
    blk_y[0] = blk[:, 0:H, :]
    blk_y[1] = blk[:, hy - H : hy, :]
    res_y[0] = right_ref[:, 0:M, :]
    res_y[1] = right_ref[:, cy - M : cy, :]
    for at, (dx, dy) in enumerate(DIAGONALS):
        bx0, by0 = (0 if dx < 0 else hx - H), (0 if dy < 0 else hy - H)
        rx0, ry0 = (0 if dx < 0 else cx - M), (0 if dy < 0 else cy - M)
        blk_c[at] = blk[bx0 : bx0 + H, by0 : by0 + H, :]
        res_c[at] = right_ref[rx0 : rx0 + M, ry0 : ry0 + M, :]

    for at, (dx, dy) in enumerate(((-1, 0), (1, 0))):
        @pl.when(jnp.logical_not(exists(dx, dy)))
        def _(at=at):
            for ref in (got_bx, got_rx, got_ix, got_fx, got_qx):
                ref[at] = jnp.zeros(ref.shape[1:], jnp.float32)

    for at, (dx, dy) in enumerate(((0, -1), (0, 1))):
        @pl.when(jnp.logical_not(exists(dx, dy)))
        def _(at=at):
            for ref in (got_by, got_ry, got_iy, got_fy, got_qy):
                ref[at] = jnp.zeros(ref.shape[1:], jnp.float32)

    for at, (dx, dy) in enumerate(DIAGONALS):
        @pl.when(jnp.logical_not(exists(dx, dy)))
        def _(at=at):
            for ref in (got_bc, got_rc, got_ic):
                ref[at] = jnp.zeros(ref.shape[1:], jnp.float32)

    diagonal_count = sum(jnp.where(exists(dx, dy), 1, 0) for dx, dy in DIAGONALS)
    pl.semaphore_wait(barrier, n_sy - 1 + n_sx - 1 + diagonal_count)

    def exchange(number, x_parts, y_parts, c_parts, got_x, got_y, got_c):
        routes = []
        for at, (dx, dy) in enumerate(((-1, 0), (1, 0))):
            routes.append((dx, dy, x_parts[at], got_x.at[1 - at], got_x.at[at], at))
        for at, (dx, dy) in enumerate(((0, -1), (0, 1))):
            routes.append((dx, dy, y_parts[at], got_y.at[1 - at], got_y.at[at], 2 + at))
        if got_c is not None:
            for at, (dx, dy) in enumerate(DIAGONALS):
                routes.append((dx, dy, c_parts[at], got_c.at[3 - at], got_c.at[at], 4 + at))
        send, recv = (halo_send, halo_recv) if got_c is not None else (face_send, face_recv)
        opposite = (1, 0, 3, 2, 7, 6, 5, 4)

        def copy(dx, dy, src, dst, slot):
            return pltpu.make_async_remote_copy(
                src_ref=src, dst_ref=dst, send_sem=send.at[number, slot],
                recv_sem=recv.at[number, opposite[slot]],
                device_id=(p + dx, q + dy), device_id_type=MESH,
            )

        for dx, dy, src, dst, mine, slot in routes:
            @pl.when(exists(dx, dy))
            def _(dx=dx, dy=dy, src=src, dst=dst, slot=slot):
                copy(dx, dy, src, dst, slot).start()

        def arrive():
            for dx, dy, src, dst, mine, slot in routes:
                @pl.when(exists(dx, dy))
                def _(dx=dx, dy=dy, src=src, mine=mine, slot=slot):
                    pltpu.make_async_remote_copy(
                        src_ref=src, dst_ref=mine, send_sem=send.at[number, slot],
                        recv_sem=recv.at[number, slot],
                        device_id=(p + dx, q + dy), device_id_type=MESH,
                    ).wait_recv()

        def leave():
            for dx, dy, src, dst, mine, slot in routes:
                @pl.when(exists(dx, dy))
                def _(dx=dx, dy=dy, src=src, dst=dst, slot=slot):
                    copy(dx, dy, src, dst, slot).wait_send()

        return arrive, leave

    def to_lines(number, source, target):
        def rows(who):
            return pl.ds(pl.multiple_of(who * cy, cy), cy)

        def copy(other, sender):
            return pltpu.make_async_remote_copy(
                src_ref=source(other), dst_ref=target(sender), send_sem=a2a_send.at[number, other],
                recv_sem=a2a_recv.at[number, sender], device_id=(p, other), device_id_type=MESH,
            )

        def begin(k, _):
            copy(lax.rem(q + k, n_sy), q).start()
            return 0

        def finish(k, _):
            other = lax.rem(q + k, n_sy)
            copy(other, q).wait_send()
            copy(other, other).wait_recv()
            return 0

        lax.fori_loop(1, n_sy, begin, 0)
        own = pltpu.make_async_copy(source(q), target(q), local_sem.at[number])
        own.start()

        def complete():
            lax.fori_loop(1, n_sy, finish, 0)
            own.wait()

        return complete

    def lines(who):
        return pl.ds(pl.multiple_of(who * cy, cy), cy)

    def half_lines(who):
        return pl.ds(pl.multiple_of(who * hy, hy), hy)

    blk_arrive, blk_leave = exchange(
        0, (blk.at[pl.ds(0, H)], blk.at[pl.ds(hx - H, H)]), (blk_y.at[0], blk_y.at[1]),
        [blk_c.at[at] for at in range(4)], got_bx, got_by, got_bc)
    res_arrive, res_leave = exchange(
        1, (right_ref.at[pl.ds(0, M)], right_ref.at[pl.ds(cx - M, M)]), (res_y.at[0], res_y.at[1]),
        [res_c.at[at] for at in range(4)], got_rx, got_ry, got_rc)
    lines_c = to_lines(
        0, lambda s: blk.at[pl.ds((s * m) // 2, mb)], lambda s: line_c.at[:, half_lines(s), :])
    lines_v = to_lines(
        1, lambda s: velocity_ref.at[:, pl.ds(s * m, m)], lambda s: line_v.at[:, :, lines(s), :])

    blk_arrive()
    wide_blk[H : H + hx, H : H + hy, :] = blk[...]
    wide_blk[0:H, H : H + hy, :] = got_bx[0]
    wide_blk[H + hx : hx + 2 * H, H : H + hy, :] = got_bx[1]
    wide_blk[H : H + hx, 0:H, :] = got_by[0]
    wide_blk[H : H + hx, H + hy : hy + 2 * H, :] = got_by[1]
    for at, (dx, dy) in enumerate(DIAGONALS):
        x0, y0 = (0 if dx < 0 else H + hx), (0 if dy < 0 else H + hy)
        wide_blk[x0 : x0 + H, y0 : y0 + H, :] = got_bc[at]
    cond[0] = jnp.zeros((ey, nz), jnp.float32)
    cond[ex // 2 + 1] = jnp.zeros((ey, nz), jnp.float32)
    for j in range(ey // 2):
        cond[1 : ex // 2 + 1, 2 * j : 2 * j + 2, :] = jnp.broadcast_to(
            wide_blk[:, j : j + 1, :], (ex // 2, 2, nz))

    row_at = lax.broadcasted_iota(jnp.int32, (ey, nz), 0)
    lane_at = lax.broadcasted_iota(jnp.int32, (ey, nz), 1)

    def coefficients(pair, _):
        before, here, after = cond[pair], cond[pair + 1], cond[pair + 2]
        yp = jnp.where(row_at < ey - 1, pltpu.roll(here, ey - 1, 0), 0.0)
        ym = jnp.where(row_at > 0, pltpu.roll(here, 1, 0), 0.0)
        zp = jnp.where(lane_at < nz - 1, pltpu.roll(here, nz - 1, 1), 0.0)
        zm = jnp.where(lane_at > 0, pltpu.roll(here, 1, 1), 0.0)
        ayp, aym = 0.5 * (here + yp), 0.5 * (here + ym)
        azp, azm = (axial_ratio * 0.5) * (here + zp), (axial_ratio * 0.5) * (here + zm)
        across = ayp + aym + azp + azm
        azp = jnp.where(lane_at < nz - 1, azp, 0.0)
        azm = jnp.where(lane_at > 0, azm, 0.0)
        for side, (xp, xm) in enumerate(((here, before), (after, here))):
            x = 2 * pair + side
            axp, axm = 0.5 * (here + xp), 0.5 * (here + xm)
            total = axp + axm + across
            inside = here > 0.0
            over = jnp.where(inside, 1.0 / jnp.where(inside, total, 1.0), 0.0)
            diag[x] = total
            inv[x] = over
            bxp[x] = axp * over
            bxm[x] = axm * over
            byp[x] = ayp * over
            bym[x] = aym * over
            bzp[x] = azp * over
            bzm[x] = azm * over
        return 0

    lax.fori_loop(0, ex // 2, coefficients, 0)

    def assemble(own, got_x, got_y, got_c):
        region[M : M + cx, M : M + cy, :] = own[...]
        region[0:M, M : M + cy, :] = got_x[0]
        region[M + cx : ex, M : M + cy, :] = got_x[1]
        region[M : M + cx, 0:M, :] = got_y[0]
        region[M : M + cx, M + cy : ey, :] = got_y[1]
        for at, (dx, dy) in enumerate(DIAGONALS):
            x0, y0 = (0 if dx < 0 else M + cx), (0 if dy < 0 else M + cy)
            region[x0 : x0 + M, y0 : y0 + M, :] = got_c[at]

    def beside(x, below, centre, above):
        total = bxp[x] * above + bxm[x] * below
        total = total + byp[x] * pltpu.roll(centre, ey - 1, 0) + bym[x] * pltpu.roll(centre, 1, 0)
        return total + bzp[x] * pltpu.roll(centre, nz - 1, 1) + bzm[x] * pltpu.roll(centre, 1, 1)

    def precondition(target):
        def begin(pair, _):
            for x in (2 * pair, 2 * pair + 1):
                start[x] = region[x] * inv[x]
            return 0

        lax.fori_loop(0, ex // 2, begin, 0)
        src = start
        for sweep in range(1, SWEEPS):
            dst = target if sweep == SWEEPS - 1 else (buf_a if sweep % 2 else buf_b)

            def body(pair, _, src=src, dst=dst, sweep=sweep):
                x = sweep + 2 * pair
                rows = [src[x - 1 + i] for i in range(4)]
                for i in range(2):
                    dst[x + i] = start[x + i] + beside(x + i, rows[i], rows[i + 1], rows[i + 2])
                return 0

            lax.fori_loop(0, (ex - 2 * sweep) // 2, body, 0)
            src = dst

    def send_faces(number, field, packed, got_x, got_y):
        packed[0] = field[M : M + cx, M : M + 1, :]
        packed[1] = field[M : M + cx, M + cy - 1 : M + cy, :]
        return exchange(
            number, (field.at[M], field.at[M + cx - 1]), (packed.at[0], packed.at[1]), None, got_x, got_y, None)

    def place_faces(field, own, got_x, got_y):
        field[M - 1] = got_x[0]
        field[M + cx] = got_x[1]
        field[M : M + cx, M - 1 : M, :] = got_y[0]
        field[M : M + cx, M + cy : M + cy + 1, :] = got_y[1]
        own[...] = field[M - 1 : M + cx + 1, M : M + cy, :]

    def operate(field, x):
        centre = field[x]
        return (diag[x] * (centre - beside(x, field[x - 1], centre, field[x + 1])))[M : M + cy, :]

    res_arrive()
    assemble(right_ref, got_rx, got_ry, got_rc)
    precondition(buf_b)
    face_arrive, face_leave = send_faces(0, buf_b, first_y, got_fx, got_fy)
    face_arrive()
    face_leave()
    place_faces(buf_b, first_own, got_fx, got_fy)

    def first_image(pair, _):
        for i in range(2):
            x = 2 * pair + i
            image[x] = operate(buf_b, M + x)
        return 0

    lax.fori_loop(0, cx // 2, first_image, 0)
    img_y[0] = image[:, 0:M, :]
    img_y[1] = image[:, cy - M : cy, :]
    for at, (dx, dy) in enumerate(DIAGONALS):
        x0, y0 = (0 if dx < 0 else cx - M), (0 if dy < 0 else cy - M)
        img_c[at] = image[x0 : x0 + M, y0 : y0 + M, :]
    img_arrive, img_leave = exchange(
        2, (image.at[pl.ds(0, M)], image.at[pl.ds(cx - M, M)]), (img_y.at[0], img_y.at[1]),
        [img_c.at[at] for at in range(4)], got_ix, got_iy, got_ic)
    lines_f = to_lines(
        2, lambda s: first_own.at[pl.ds(s * m, m + 2)], lambda s: line_f.at[:, lines(s), :])

    img_arrive()
    assemble(image, got_ix, got_iy, got_ic)
    precondition(buf_q)
    q_arrive, q_leave = send_faces(1, buf_q, q_y, got_qx, got_qy)
    q_arrive()
    q_leave()
    place_faces(buf_q, q_own, got_qx, got_qy)
    lines_q = to_lines(
        3, lambda s: q_own.at[pl.ds(s * m, m + 2)], lambda s: line_q.at[:, lines(s), :])

    def products(x, carry):
        ri, ii, wi, ww, rw = carry
        r, i, w = right_ref[x], image[x], operate(buf_q, M + x)
        return ri + r * i, ii + i * i, wi + w * i, ww + w * w, rw + r * w

    zero = jnp.zeros((cy, nz), jnp.float32)
    totals = lax.fori_loop(0, cx, products, (zero,) * 5)
    packed = jnp.zeros((8, nz), jnp.float32)
    row8 = lax.broadcasted_iota(jnp.int32, (8, nz), 0)
    for at, total in enumerate(totals):
        packed = jnp.where(row8 == at, jnp.sum(total, axis=0, keepdims=True), packed)
    sums_mine[...] = packed

    def gather(axis_at, count, mine, slots, send, recv, device):
        def copy(other, sender):
            return pltpu.make_async_remote_copy(
                src_ref=mine, dst_ref=slots.at[sender], send_sem=send.at[other],
                recv_sem=recv.at[sender], device_id=device(other), device_id_type=MESH)

        def begin(k, _):
            copy(lax.rem(axis_at + k, count), axis_at).start()
            return 0

        def finish(k, _):
            other = lax.rem(axis_at + k, count)
            copy(other, axis_at).wait_send()
            copy(other, other).wait_recv()
            return 0

        lax.fori_loop(1, count, begin, 0)
        slots[axis_at] = mine[...]

        def complete():
            lax.fori_loop(1, count, finish, 0)
            return jnp.sum(slots[...], axis=0)

        return complete

    row_sums = gather(p, n_sx, sums_mine, sums_x, sx_send, sx_recv, lambda other: (other, q))
    lines_v()
    lines_c()
    lines_f()
    matrix = matrix_ref[...]
    for row in range(m):
        next_ref[2, row] = jnp.dot(
            matrix, line_v[2, row], precision=highest, preferred_element_type=jnp.float32)
    sums_row[...] = row_sums()
    all_sums = gather(q, n_sy, sums_row, sums_y, sy_send, sy_recv, lambda other: (p, other))
    blk_leave()
    res_leave()
    img_leave()
    scalars = jnp.sum(all_sums(), axis=1, keepdims=True)
    ri, ii, wi, ww, rw = (scalars[at : at + 1, :] for at in range(5))
    alpha = ri / ii
    gamma = wi / ii
    kappa = (gamma * ri - rw) / (ww - gamma * wi)
    of_first = alpha + kappa * gamma

    def own_potential(x, _):
        potential_ref[x] = of_first * first_own[x + 1] - kappa * q_own[x + 1]
        return 0

    lax.fori_loop(0, cx, own_potential, 0)

    lines_q()
    line_at = lax.broadcasted_iota(jnp.int32, (lines_count, nz), 0)
    planes = [of_first * line_f[row] - kappa * line_q[row] for row in range(m + 2)]
    for row in range(m):
        here = planes[row + 1]
        grad_x = 0.5 * (planes[row + 2] - planes[row])
        up = jnp.where(line_at < lines_count - 1, pltpu.roll(here, lines_count - 1, 0), 0.0)
        down = jnp.where(line_at > 0, pltpu.roll(here, 1, 0), 0.0)
        grad_y = 0.5 * (up - down)
        compact = line_c[row // 2]
        c = coupling * jnp.broadcast_to(
            compact[:, None, :], (lines_count // 2, 2, nz)).reshape(lines_count, nz)
        vx, vy = line_v[0, row], line_v[1, row]
        next_ref[0, row] = jnp.dot(
            matrix, vx + c * (-grad_y - vx), precision=highest, preferred_element_type=jnp.float32)
        next_ref[1, row] = jnp.dot(
            matrix, vy + c * (grad_x - vy), precision=highest, preferred_element_type=jnp.float32)


def per_device(n_sx, n_sy, right_side, class_map, conductivity_table, velocity):
    cx, cy, nz = right_side.shape
    m = cx // n_sy
    assert m * n_sy == cx and (m == 1 or m % 2 == 0)
    mb = max(1, m // 2)
    hx, hy = cx // 2, cy // 2
    M, H = MARGIN, MARGIN // 2
    ex, ey = cx + 2 * M, cy + 2 * M
    ny = cy * n_sy
    matrix = jnp.asarray(line_matrix(ny, cy))

    def vmem(*shape):
        return pltpu.VMEM(shape, jnp.float32)

    wide = vmem(ex, ey, nz)
    whole = pl.BlockSpec(memory_space=pltpu.VMEM)
    dma = pltpu.SemaphoreType.DMA
    scratch = [
        vmem(hx, hy, nz), vmem(2, hx, H, nz), vmem(4, H, H, nz),
        vmem(2, H, hy, nz), vmem(2, hx, H, nz), vmem(4, H, H, nz),
        vmem(ex // 2, ey // 2, nz), vmem(ex // 2 + 2, ey, nz),
        vmem(2, cx, M, nz), vmem(4, M, M, nz),
        vmem(2, M, cy, nz), vmem(2, cx, M, nz), vmem(4, M, M, nz),
        vmem(2, cx, M, nz), vmem(4, M, M, nz),
        vmem(2, M, cy, nz), vmem(2, cx, M, nz), vmem(4, M, M, nz),
        vmem(2, cx, 1, nz), vmem(2, ey, nz), vmem(2, cx, 1, nz),
        vmem(2, cx, 1, nz), vmem(2, ey, nz), vmem(2, cx, 1, nz),
        wide, wide, wide, wide, wide,
        wide, wide, wide, wide, wide, wide, wide, wide,
        vmem(cx + 2, cy, nz), vmem(cx, cy, nz), vmem(cx + 2, cy, nz),
        vmem(3, m, ny, nz), vmem(mb, ny // 2, nz), vmem(m + 2, ny, nz), vmem(m + 2, ny, nz),
        vmem(8, nz), vmem(n_sx, 8, nz), vmem(8, nz), vmem(n_sy, 8, nz),
        dma((3, 8)), dma((3, 8)), dma((2, 8)), dma((2, 8)),
        dma((4, n_sy)), dma((4, n_sy)), dma((4,)),
        dma((n_sx,)), dma((n_sx,)), dma((n_sy,)), dma((n_sy,)),
    ]
    return pl.pallas_call(
        functools.partial(kernel, n_sx, n_sy),
        out_shape=(
            jax.ShapeDtypeStruct((cx, cy, nz), jnp.float32),
            jax.ShapeDtypeStruct((3, m, ny, nz), jnp.float32),
        ),
        in_specs=[
            whole, whole, pl.BlockSpec(memory_space=pltpu.SMEM),
            pl.BlockSpec(memory_space=pl.ANY), whole,
        ],
        out_specs=(whole, whole),
        scratch_shapes=scratch,
        compiler_params=pltpu.CompilerParams(
            collective_id=0, has_side_effects=True, vmem_limit_bytes=40 * 2**20),
    )(right_side, class_map, conductivity_table, velocity, matrix)


def solution(mesh):
    return jax.shard_map(
        functools.partial(per_device, mesh.shape["sx"], mesh.shape["sy"]),
        mesh=mesh,
        in_specs=(P("sx", "sy", None), P("sx", "sy", None), P(), P(None, "sx", "sy", None)),
        out_specs=(P("sx", "sy", None), P(None, ("sx", "sy"), None, None)),
        check_vma=False,
    )
```

time: 263 us -> 54.1 us (0.21)
  blocking collectives: 131 us -> 0 us
  starting transfers between devices: 67.9 us -> 0 us
  Pallas kernels: 0 us -> 47.2 us
  waiting for transfers between devices: 32.4 us -> 0 us
  other arithmetic: 17.9 us -> 0 us
  between operations: 5.52 us -> 0.65 us
  matrix products: 3.08 us -> 0 us
    psum x3 -> x0, blocking collectives: 131 us -> none  [global_sums(): return lax.psum(jnp.stack(partial_terms), ('sx', 'sy'))]
    ppermute x24 -> x0, starting transfers between devices: 61.6 us -> none  [the longest x12 45.9 us: with_halo(): before = lax.ppermute(last, axis, up)]
    pallas_call x0 -> x1, Pallas kernels: none -> 47.2 us  [per_device(): pl.pallas_call(functools.partial(kernel, n_sx, n_sy), out_shape=(jax.Shap...]
    ppermute x24 -> x0, waiting for transfers between devices: 19.9 us -> none  [the longest x12 14.5 us: with_halo(): after = lax.ppermute(initial, axis, down)]
    all_to_all x1 -> x0, waiting for transfers between devices: 12.5 us -> none  [per_device(): lax.all_to_all(moved_velocity, 'sy', split_axis=1, concat_axis=2, tiled=T...]
    all_to_all x1 -> x0, starting transfers between devices: 6.28 us -> none  [per_device(): lax.all_to_all(moved_velocity, 'sy', split_axis=1, concat_axis=2, tiled=T...]
    unnamed x42 -> x12, local copies, waits for them, and re-layouts: 0.12 us -> 5.99 us
    add x10 -> x0, other arithmetic: 5.57 us -> none  [the longest x8 4.48 us: precondition(): update + (region - apply_operator(local_faces, local_diagonal, spatial_pa...]
  transfers between devices with their start and end apart: 25 -> 0, of which waited for: 11 -> 0; matrix products, arithmetic and copies ran while one was open for 1% -> 0% of each run, Pallas kernels for 0% -> 0%
where the time goes in v1:
time: 54.1 us; the launch traced here: 53.8 us
  Pallas kernels  47.2 us (87%)
  local copies, waits for them, and re-layouts  5.99 us (11%)
  between operations  0.65 us (1%)
    pallas_call x1, Pallas kernels, per_device(): pl.pallas_call(functools.partial(kernel, n_sx, n_sy), out_shape=(jax.Shap...  47.2 us
    unnamed x12, local copies, waits for them, and re-layouts  5.99 us

profile of v1, /device:TPU:0, one launch (start us, length us, event | category | flops | bytes accessed | tf_op | source)
XLA Modules:
  0.0 53.8 jit_solution(9424968745151090229)
XLA Ops:
  0.6 0.0 copy-start
  0.6 1.1 %copy-done = f32[3,32,16,128]{3,2,1,0:T(8,128)S(1)} copy-done((f32[3,32,16,128]{3,2,1,0:T(8,128)S(1)}, f32[3,32,16,128]{3,2,1,0:T(8,128)}, u32[]{:S(2)}) %copy-start) | copy-done | bytes 786456
  1.8 0.0 copy-start.1
  1.8 0.9 %copy-done.1 = f32[32,16,128]{2,1,0:T(8,128)S(1)} copy-done((f32[32,16,128]{2,1,0:T(8,128)S(1)}, f32[32,16,128]{2,1,0:T(8,128)}, u32[]{:S(2)}) %copy-start.1) | copy-done | bytes 262168
  2.7 0.0 copy-start.2
  2.7 0.8 %copy-done.2 = s32[16,8,32]{2,1,0:T(8,128)S(1)} copy-done((s32[16,8,32]{2,1,0:T(8,128)S(1)}, s32[16,8,32]{2,1,0:T(8,128)}, u32[]{:S(2)}) %copy-start.2) | copy-done | bytes 16408
  3.6 0.0 copy-start.3
  3.6 0.8 %copy-done.3 = f32[128,128]{1,0:T(8,128)S(1)} copy-done((f32[128,128]{1,0:T(8,128)S(1)}, f32[128,128]{1,0:T(8,128)}, u32[]{:S(2)}) %copy-start.3) | copy-done | bytes 65560
  4.4 0.0 copy-start.4
  4.4 0.7 %copy-done.4 = f32[8]{0:T(128)S(1)} copy-done((f32[8]{0:T(128)S(1)}, f32[8]{0:T(128)}, u32[]{:S(2)}) %copy-start.4) | copy-done | bytes 56
  5.1 47.2 %shard_map.68 = (f32[32,16,128]{2,1,0:T(8,128)S(1)}, f32[3,4,128,128]{3,2,1,0:T(8,128)S(1)}) custom-call(f32[32,16,128]{2,1,0:T(8,128)S(1)} %copy-done.1, s32[16,8,32]{2,1,0:T(8,128)S(1)} %copy-done.2, f32[8]{0:T(128)S(1)} %copy-done.4, f32[3,32,16,128]{3,2,1,0:T(8,128)S(1)} %copy-done, f32[128,128]{1,0:T(8,128)S(1)} %copy-done.3), custom_call_target="tpu_custom_call" | custom-call | tf_op jit(solution)/shard_map/pallas_call | solution.py:465
  52.2 0.7 %copy.9 = f32[32,16,128]{2,1,0:T(8,128)} copy(f32[32,16,128]{2,1,0:T(8,128)S(1)} %get-tuple-element.4) | data formatting | bytes 524288
  52.9 0.9 %copy.10 = f32[3,4,128,128]{3,2,1,0:T(8,128)} copy(f32[3,4,128,128]{3,2,1,0:T(8,128)S(1)} %get-tuple-element.5) | data formatting | bytes 1572864
Async XLA Ops:
  0.6 1.1 %copy-start = (f32[3,32,16,128]{3,2,1,0:T(8,128)S(1)}, f32[3,32,16,128]{3,2,1,0:T(8,128)}, u32[]{:S(2)}) copy-start(f32[3,32,16,128]{3,2,1,0:T(8,128)} %velocity_ref.1) | copy-start | bytes 2359300
  1.8 0.9 %copy-start.1 = (f32[32,16,128]{2,1,0:T(8,128)S(1)}, f32[32,16,128]{2,1,0:T(8,128)}, u32[]{:S(2)}) copy-start(f32[32,16,128]{2,1,0:T(8,128)} %right_ref.1) | copy-start | bytes 786436
  2.7 0.8 %copy-start.2 = (s32[16,8,32]{2,1,0:T(8,128)S(1)}, s32[16,8,32]{2,1,0:T(8,128)}, u32[]{:S(2)}) copy-start(s32[16,8,32]{2,1,0:T(8,128)} %class_ref.1) | copy-start | bytes 49156
  3.6 0.8 %copy-start.3 = (f32[128,128]{1,0:T(8,128)S(1)}, f32[128,128]{1,0:T(8,128)}, u32[]{:S(2)}) copy-start(f32[128,128]{1,0:T(8,128)} %constant.2.clone.matrix_ref) | copy-start | bytes 196612
  4.4 0.7 %copy-start.4 = (f32[8]{0:T(128)S(1)}, f32[8]{0:T(128)}, u32[]{:S(2)}) copy-start(f32[8]{0:T(128)} %table_ref.1) | copy-start | bytes 100

commit v2 on v1

--- a/solution.py
+++ b/solution.py
@@ -30,8 +30,10 @@
 
 
 def kernel(
-    n_sx, n_sy, right_ref, class_ref, table_ref, velocity_ref, matrix_ref,
-    potential_ref, next_ref,
+    n_sx, n_sy, right_hbm, class_hbm, table_hbm, velocity_ref, matrix_hbm,
+    potential_hbm, next_hbm,
+    potential_ref, next_ref, store_sem,
+    right_ref, class_ref, table_ref, matrix_ref, load_sem,
     blk, blk_y, blk_c, got_bx, got_by, got_bc, wide_blk, cond,
     res_y, res_c, got_rx, got_ry, got_rc,
     img_y, img_c, got_ix, got_iy, got_ic,
@@ -61,6 +63,14 @@
                 ok = this if ok is None else ok & this
         return ok
 
+    loads = [
+        pltpu.make_async_copy(src, dst, load_sem.at[at])
+        for at, (src, dst) in enumerate((
+            (class_hbm, class_ref), (table_hbm, table_ref), (right_hbm, right_ref), (matrix_hbm, matrix_ref)))
+    ]
+    for load in loads:
+        load.start()
+
     barrier = pltpu.get_barrier_semaphore()
 
     def greet_y(k, _):
@@ -78,6 +88,8 @@
         def _(dx=dx, dy=dy):
             pl.semaphore_signal(barrier, inc=1, device_id=(p + dx, q + dy), device_id_type=MESH)
 
+    loads[0].wait()
+    loads[1].wait()
     classes = class_ref[...].reshape(hx * hy, class_ref.shape[2])
     picked = jnp.zeros(classes.shape, jnp.float32)
     for one in range(CLASSES):
@@ -89,6 +101,7 @@
     blk[...] = jnp.dot(picked, spread, precision=highest, preferred_element_type=jnp.float32).reshape(hx, hy, nz)
     blk_y[0] = blk[:, 0:H, :]
     blk_y[1] = blk[:, hy - H : hy, :]
+    loads[2].wait()
     res_y[0] = right_ref[:, 0:M, :]
     res_y[1] = right_ref[:, cy - M : cy, :]
     for at, (dx, dy) in enumerate(DIAGONALS):
@@ -225,7 +238,7 @@
     row_at = lax.broadcasted_iota(jnp.int32, (ey, nz), 0)
     lane_at = lax.broadcasted_iota(jnp.int32, (ey, nz), 1)
 
-    def coefficients(pair, _):
+    def coefficients(pair):
         before, here, after = cond[pair], cond[pair + 1], cond[pair + 2]
         yp = jnp.where(row_at < ey - 1, pltpu.roll(here, ey - 1, 0), 0.0)
         ym = jnp.where(row_at > 0, pltpu.roll(here, 1, 0), 0.0)
@@ -250,9 +263,9 @@
             bym[x] = aym * over
             bzp[x] = azp * over
             bzm[x] = azm * over
-        return 0
-
-    lax.fori_loop(0, ex // 2, coefficients, 0)
+
+    for pair in range(ex // 2):
+        coefficients(pair)
 
     def assemble(own, got_x, got_y, got_c):
         region[M : M + cx, M : M + cy, :] = own[...]
@@ -270,24 +283,17 @@
         return total + bzp[x] * pltpu.roll(centre, nz - 1, 1) + bzm[x] * pltpu.roll(centre, 1, 1)
 
     def precondition(target):
-        def begin(pair, _):
-            for x in (2 * pair, 2 * pair + 1):
-                start[x] = region[x] * inv[x]
-            return 0
-
-        lax.fori_loop(0, ex // 2, begin, 0)
+        for x in range(ex):
+            start[x] = region[x] * inv[x]
         src = start
         for sweep in range(1, SWEEPS):
             dst = target if sweep == SWEEPS - 1 else (buf_a if sweep % 2 else buf_b)
 
-            def body(pair, _, src=src, dst=dst, sweep=sweep):
-                x = sweep + 2 * pair
-                rows = [src[x - 1 + i] for i in range(4)]
-                for i in range(2):
-                    dst[x + i] = start[x + i] + beside(x + i, rows[i], rows[i + 1], rows[i + 2])
-                return 0
-
-            lax.fori_loop(0, (ex - 2 * sweep) // 2, body, 0)
+            below, centre = src[sweep - 1], src[sweep]
+            for x in range(sweep, ex - sweep):
+                above = src[x + 1]
+                dst[x] = start[x] + beside(x, below, centre, above)
+                below, centre = centre, above
             src = dst
 
     def send_faces(number, field, packed, got_x, got_y):
@@ -315,13 +321,8 @@
     face_leave()
     place_faces(buf_b, first_own, got_fx, got_fy)
 
-    def first_image(pair, _):
-        for i in range(2):
-            x = 2 * pair + i
-            image[x] = operate(buf_b, M + x)
-        return 0
-
-    lax.fori_loop(0, cx // 2, first_image, 0)
+    for x in range(cx):
+        image[x] = operate(buf_b, M + x)
     img_y[0] = image[:, 0:M, :]
     img_y[1] = image[:, cy - M : cy, :]
     for at, (dx, dy) in enumerate(DIAGONALS):
@@ -349,7 +350,9 @@
         return ri + r * i, ii + i * i, wi + w * i, ww + w * w, rw + r * w
 
     zero = jnp.zeros((cy, nz), jnp.float32)
-    totals = lax.fori_loop(0, cx, products, (zero,) * 5)
+    totals = (zero,) * 5
+    for x in range(cx):
+        totals = products(x, totals)
     packed = jnp.zeros((8, nz), jnp.float32)
     row8 = lax.broadcasted_iota(jnp.int32, (8, nz), 0)
     for at, total in enumerate(totals):
@@ -385,10 +388,22 @@
     lines_v()
     lines_c()
     lines_f()
+    loads[3].wait()
     matrix = matrix_ref[...]
+    high = matrix.astype(jnp.bfloat16)
+    low = (matrix - high.astype(jnp.float32)).astype(jnp.bfloat16)
+    factors = jnp.concatenate([high, high, low], axis=1)
+
+    def diffuse(field):
+        coarse = field.astype(jnp.bfloat16)
+        fine = (field - coarse.astype(jnp.float32)).astype(jnp.bfloat16)
+        return jnp.dot(
+            factors, jnp.concatenate([coarse, fine, coarse], axis=0), preferred_element_type=jnp.float32)
+
     for row in range(m):
-        next_ref[2, row] = jnp.dot(
-            matrix, line_v[2, row], precision=highest, preferred_element_type=jnp.float32)
+        next_ref[2, row] = diffuse(line_v[2, row])
+    stores = [pltpu.make_async_copy(next_ref.at[2], next_hbm.at[2], store_sem.at[2])]
+    stores[-1].start()
     sums_row[...] = row_sums()
     all_sums = gather(q, n_sy, sums_row, sums_y, sy_send, sy_recv, lambda other: (p, other))
     blk_leave()
@@ -401,11 +416,10 @@
     kappa = (gamma * ri - rw) / (ww - gamma * wi)
     of_first = alpha + kappa * gamma
 
-    def own_potential(x, _):
+    for x in range(cx):
         potential_ref[x] = of_first * first_own[x + 1] - kappa * q_own[x + 1]
-        return 0
-
-    lax.fori_loop(0, cx, own_potential, 0)
+    stores.append(pltpu.make_async_copy(potential_ref, potential_hbm, store_sem.at[0]))
+    stores[-1].start()
 
     lines_q()
     line_at = lax.broadcasted_iota(jnp.int32, (lines_count, nz), 0)
@@ -420,10 +434,14 @@
         c = coupling * jnp.broadcast_to(
             compact[:, None, :], (lines_count // 2, 2, nz)).reshape(lines_count, nz)
         vx, vy = line_v[0, row], line_v[1, row]
-        next_ref[0, row] = jnp.dot(
-            matrix, vx + c * (-grad_y - vx), precision=highest, preferred_element_type=jnp.float32)
-        next_ref[1, row] = jnp.dot(
-            matrix, vy + c * (grad_x - vy), precision=highest, preferred_element_type=jnp.float32)
+        next_ref[0, row] = diffuse(vx + c * (-grad_y - vx))
+        next_ref[1, row] = diffuse(vy + c * (grad_x - vy))
+        both = pl.ds(0, 2)
+        stores.append(pltpu.make_async_copy(
+            next_ref.at[both, row], next_hbm.at[both, row], store_sem.at[3 + row]))
+        stores[-1].start()
+    for store in stores:
+        store.wait()
 
 
 def per_device(n_sx, n_sy, right_side, class_map, conductivity_table, velocity):
@@ -441,9 +459,11 @@
         return pltpu.VMEM(shape, jnp.float32)
 
     wide = vmem(ex, ey, nz)
-    whole = pl.BlockSpec(memory_space=pltpu.VMEM)
     dma = pltpu.SemaphoreType.DMA
     scratch = [
+        vmem(cx, cy, nz), vmem(3, m, ny, nz), dma((3 + m,)),
+        vmem(cx, cy, nz), pltpu.VMEM(class_map.shape, jnp.int32),
+        pltpu.SMEM(conductivity_table.shape, jnp.float32), vmem(ny, ny), dma((4,)),
         vmem(hx, hy, nz), vmem(2, hx, H, nz), vmem(4, H, H, nz),
         vmem(2, H, hy, nz), vmem(2, hx, H, nz), vmem(4, H, H, nz),
         vmem(ex // 2, ey // 2, nz), vmem(ex // 2 + 2, ey, nz),
@@ -468,14 +488,11 @@
             jax.ShapeDtypeStruct((cx, cy, nz), jnp.float32),
             jax.ShapeDtypeStruct((3, m, ny, nz), jnp.float32),
         ),
-        in_specs=[
-            whole, whole, pl.BlockSpec(memory_space=pltpu.SMEM),
-            pl.BlockSpec(memory_space=pl.ANY), whole,
-        ],
-        out_specs=(whole, whole),
+        in_specs=[pl.BlockSpec(memory_space=pltpu.MemorySpace.HBM)] * 5,
+        out_specs=(pl.BlockSpec(memory_space=pltpu.MemorySpace.HBM),) * 2,
         scratch_shapes=scratch,
         compiler_params=pltpu.CompilerParams(
-            collective_id=0, has_side_effects=True, vmem_limit_bytes=40 * 2**20),
+            collective_id=0, has_side_effects=True, vmem_limit_bytes=61 * 2**20),
     )(right_side, class_map, conductivity_table, velocity, matrix)
 
 

time: 54.1 us -> 42.4 us (0.78)
  Pallas kernels: 47.2 us -> 37.8 us
  local copies, waits for them, and re-layouts: 5.99 us -> 3.73 us
    pallas_call x1, Pallas kernels: 47.2 us -> 37.8 us  [per_device(): pl.pallas_call(functools.partial(kernel, n_sx, n_sy), out_shape=(jax.Shap...]
    unnamed x12 -> x2, local copies, waits for them, and re-layouts: 5.99 us -> 3.73 us
where the time goes in v2:
time: 42.4 us; the launch traced here: 42.2 us
  Pallas kernels  37.8 us (89%)
  local copies, waits for them, and re-layouts  3.73 us (9%)
  between operations  0.64 us (2%)
    pallas_call x1, Pallas kernels, per_device(): pl.pallas_call(functools.partial(kernel, n_sx, n_sy), out_shape=(jax.Shap...  37.8 us
    unnamed x2, local copies, waits for them, and re-layouts  3.73 us

profile of v2, /device:TPU:0, one launch (start us, length us, event | category | flops | bytes accessed | tf_op | source)
XLA Modules:
  0.0 42.2 jit_solution(5301539085270901204)
XLA Ops:
  0.6 37.8 %shard_map.68 = (f32[32,16,128]{2,1,0:T(8,128)}, f32[3,4,128,128]{3,2,1,0:T(8,128)}) custom-call(f32[32,16,128]{2,1,0:T(8,128)} %right_hbm.1, s32[16,8,32]{2,1,0:T(8,128)} %class_hbm.1, f32[8]{0:T(128)} %table_hbm.1, f32[3,32,16,128]{3,2,1,0:T(8,128)} %velocity_ref.1, f32[128,128]{1,0:T(8,128)} %constant.2.clone.matrix_hbm), custom_call_target="tpu_custom_call" | custom-call | tf_op jit(solution)/shard_map/pallas_call | solution.py:485
  38.5 1.7 %copy.9 = f32[32,16,128]{2,1,0:T(8,128)} copy(f32[32,16,128]{2,1,0:T(8,128)} %get-tuple-element.4) | data formatting | bytes 524288
  40.1 2.1 %copy.10 = f32[3,4,128,128]{3,2,1,0:T(8,128)} copy(f32[3,4,128,128]{3,2,1,0:T(8,128)} %get-tuple-element.5) | data formatting | bytes 1572864

commit v3 on v2

--- a/solution.py
+++ b/solution.py
@@ -31,8 +31,7 @@
 
 def kernel(
     n_sx, n_sy, right_hbm, class_hbm, table_hbm, velocity_ref, matrix_hbm,
-    potential_hbm, next_hbm,
-    potential_ref, next_ref, store_sem,
+    potential_ref, next_ref,
     right_ref, class_ref, table_ref, matrix_ref, load_sem,
     blk, blk_y, blk_c, got_bx, got_by, got_bc, wide_blk, cond,
     res_y, res_c, got_rx, got_ry, got_rc,
@@ -44,6 +43,7 @@
     line_v, line_c, line_f, line_q, sums_mine, sums_x, sums_row, sums_y,
     halo_send, halo_recv, face_send, face_recv, a2a_send, a2a_recv, local_sem,
     sx_send, sx_recv, sy_send, sy_recv,
+    force_f, force_q, edge_mine, edge_got, edge_send, edge_recv,
 ):
     p, q = lax.axis_index("sx"), lax.axis_index("sy")
     cx, cy, nz = right_ref.shape
@@ -307,7 +307,23 @@
         field[M + cx] = got_x[1]
         field[M : M + cx, M - 1 : M, :] = got_y[0]
         field[M : M + cx, M + cy : M + cy + 1, :] = got_y[1]
-        own[...] = field[M - 1 : M + cx + 1, M : M + cy, :]
+        if own is not None:
+            own[...] = field[M - 1 : M + cx + 1, M : M + cy, :]
+
+    def shift_of(rows):
+        at = lax.broadcasted_iota(jnp.int32, rows.shape, 0)
+        up = jnp.where(at < lines_count - 1, pltpu.roll(rows, lines_count - 1, 0), 0.0)
+        return 0.5 * (up - jnp.where(at > 0, pltpu.roll(rows, 1, 0), 0.0))
+
+    def factor(row):
+        return coupling * jnp.broadcast_to(
+            line_c[row // 2][:, None, :], (lines_count // 2, 2, nz)).reshape(lines_count, nz)
+
+    def forces(planes, target):
+        for row in range(m):
+            c = factor(row)
+            target[0, row] = diffuse(c * -shift_of(planes[row + 1]))
+            target[1, row] = diffuse(c * (0.5 * (planes[row + 2] - planes[row])))
 
     def operate(field, x):
         centre = field[x]
@@ -334,15 +350,78 @@
     lines_f = to_lines(
         2, lambda s: first_own.at[pl.ds(s * m, m + 2)], lambda s: line_f.at[:, lines(s), :])
 
+    loads[3].wait()
+    matrix = matrix_ref[...]
+    high = matrix.astype(jnp.bfloat16)
+    low = (matrix - high.astype(jnp.float32)).astype(jnp.bfloat16)
+    factors = jnp.concatenate([high, high, low], axis=1)
+
+    def diffuse(field):
+        coarse = field.astype(jnp.bfloat16)
+        fine = (field - coarse.astype(jnp.float32)).astype(jnp.bfloat16)
+        return jnp.dot(
+            factors, jnp.concatenate([coarse, fine, coarse], axis=0), preferred_element_type=jnp.float32)
+
+    lines_v()
+    lines_c()
+    for row in range(m):
+        c, vx, vy = factor(row), line_v[0, row], line_v[1, row]
+        next_ref[0, row] = diffuse(vx - c * vx)
+        next_ref[1, row] = diffuse(vy - c * vy)
+        next_ref[2, row] = diffuse(line_v[2, row])
+
     img_arrive()
     assemble(image, got_ix, got_iy, got_ic)
     precondition(buf_q)
     q_arrive, q_leave = send_faces(1, buf_q, q_y, got_qx, got_qy)
+    q_own[0] = jnp.zeros((cy, nz), jnp.float32)
+    q_own[cx + 1] = jnp.zeros((cy, nz), jnp.float32)
+    q_own[1 : cx + 1] = buf_q[M : M + cx, M : M + cy, :]
+    lines_q = to_lines(
+        3, lambda s: q_own.at[pl.ds(s * m, m + 2)], lambda s: line_q.at[:, lines(s), :])
+    lines_f()
+    forces([line_f[row] for row in range(m + 2)], force_f)
     q_arrive()
     q_leave()
-    place_faces(buf_q, q_own, got_qx, got_qy)
-    lines_q = to_lines(
-        3, lambda s: q_own.at[pl.ds(s * m, m + 2)], lambda s: line_q.at[:, lines(s), :])
+    place_faces(buf_q, None, got_qx, got_qy)
+
+    edge_mine[0] = got_qx[0, M : M + cy, :]
+    edge_mine[1] = got_qx[1, M : M + cy, :]
+
+    def edge_copy(side, target, sender):
+        return pltpu.make_async_remote_copy(
+            src_ref=edge_mine.at[side], dst_ref=edge_got.at[lines(sender), :],
+            send_sem=edge_send.at[side], recv_sem=edge_recv.at[sender],
+            device_id=(p, target), device_id_type=MESH)
+
+    ends = (0, n_sy - 1)
+    for side, end in enumerate(ends):
+        @pl.when(q != end)
+        def _(side=side, end=end):
+            edge_copy(side, end, q).start()
+
+        @pl.when(q == end)
+        def _(side=side):
+            edge_got[lines(q), :] = edge_mine[side]
+
+    def edges():
+        for side, end in enumerate(ends):
+            @pl.when(q != end)
+            def _(side=side, end=end):
+                edge_copy(side, end, q).wait_send()
+
+            @pl.when(q == end)
+            def _(side=side):
+                def finish(k, _):
+                    other = lax.rem(q + k, n_sy)
+                    edge_copy(side, other, other).wait_recv()
+                    return 0
+
+                lax.fori_loop(1, n_sy, finish, 0)
+
+        @pl.when((q != 0) & (q != n_sy - 1))
+        def _():
+            edge_got[...] = jnp.zeros((lines_count, nz), jnp.float32)
 
     def products(x, carry):
         ri, ii, wi, ww, rw = carry
@@ -385,30 +464,17 @@
         return complete
 
     row_sums = gather(p, n_sx, sums_mine, sums_x, sx_send, sx_recv, lambda other: (other, q))
-    lines_v()
-    lines_c()
-    lines_f()
-    loads[3].wait()
-    matrix = matrix_ref[...]
-    high = matrix.astype(jnp.bfloat16)
-    low = (matrix - high.astype(jnp.float32)).astype(jnp.bfloat16)
-    factors = jnp.concatenate([high, high, low], axis=1)
-
-    def diffuse(field):
-        coarse = field.astype(jnp.bfloat16)
-        fine = (field - coarse.astype(jnp.float32)).astype(jnp.bfloat16)
-        return jnp.dot(
-            factors, jnp.concatenate([coarse, fine, coarse], axis=0), preferred_element_type=jnp.float32)
-
-    for row in range(m):
-        next_ref[2, row] = diffuse(line_v[2, row])
-    stores = [pltpu.make_async_copy(next_ref.at[2], next_hbm.at[2], store_sem.at[2])]
-    stores[-1].start()
     sums_row[...] = row_sums()
     all_sums = gather(q, n_sy, sums_row, sums_y, sy_send, sy_recv, lambda other: (p, other))
     blk_leave()
     res_leave()
     img_leave()
+    lines_q()
+    edges()
+    planes = [line_q[row] for row in range(m + 2)]
+    planes[0] = jnp.where(q == 0, edge_got[...], planes[0])
+    planes[m + 1] = jnp.where(q == n_sy - 1, edge_got[...], planes[m + 1])
+    forces(planes, force_q)
     scalars = jnp.sum(all_sums(), axis=1, keepdims=True)
     ri, ii, wi, ww, rw = (scalars[at : at + 1, :] for at in range(5))
     alpha = ri / ii
@@ -418,30 +484,10 @@
 
     for x in range(cx):
         potential_ref[x] = of_first * first_own[x + 1] - kappa * q_own[x + 1]
-    stores.append(pltpu.make_async_copy(potential_ref, potential_hbm, store_sem.at[0]))
-    stores[-1].start()
-
-    lines_q()
-    line_at = lax.broadcasted_iota(jnp.int32, (lines_count, nz), 0)
-    planes = [of_first * line_f[row] - kappa * line_q[row] for row in range(m + 2)]
+
     for row in range(m):
-        here = planes[row + 1]
-        grad_x = 0.5 * (planes[row + 2] - planes[row])
-        up = jnp.where(line_at < lines_count - 1, pltpu.roll(here, lines_count - 1, 0), 0.0)
-        down = jnp.where(line_at > 0, pltpu.roll(here, 1, 0), 0.0)
-        grad_y = 0.5 * (up - down)
-        compact = line_c[row // 2]
-        c = coupling * jnp.broadcast_to(
-            compact[:, None, :], (lines_count // 2, 2, nz)).reshape(lines_count, nz)
-        vx, vy = line_v[0, row], line_v[1, row]
-        next_ref[0, row] = diffuse(vx + c * (-grad_y - vx))
-        next_ref[1, row] = diffuse(vy + c * (grad_x - vy))
-        both = pl.ds(0, 2)
-        stores.append(pltpu.make_async_copy(
-            next_ref.at[both, row], next_hbm.at[both, row], store_sem.at[3 + row]))
-        stores[-1].start()
-    for store in stores:
-        store.wait()
+        for part in range(2):
+            next_ref[part, row] += of_first * force_f[part, row] - kappa * force_q[part, row]
 
 
 def per_device(n_sx, n_sy, right_side, class_map, conductivity_table, velocity):
@@ -461,7 +507,6 @@
     wide = vmem(ex, ey, nz)
     dma = pltpu.SemaphoreType.DMA
     scratch = [
-        vmem(cx, cy, nz), vmem(3, m, ny, nz), dma((3 + m,)),
         vmem(cx, cy, nz), pltpu.VMEM(class_map.shape, jnp.int32),
         pltpu.SMEM(conductivity_table.shape, jnp.float32), vmem(ny, ny), dma((4,)),
         vmem(hx, hy, nz), vmem(2, hx, H, nz), vmem(4, H, H, nz),
@@ -481,15 +526,16 @@
         dma((3, 8)), dma((3, 8)), dma((2, 8)), dma((2, 8)),
         dma((4, n_sy)), dma((4, n_sy)), dma((4,)),
         dma((n_sx,)), dma((n_sx,)), dma((n_sy,)), dma((n_sy,)),
+        vmem(2, m, ny, nz), vmem(2, m, ny, nz), vmem(2, cy, nz), vmem(ny, nz), dma((2,)), dma((n_sy,)),
     ]
     return pl.pallas_call(
         functools.partial(kernel, n_sx, n_sy),
         out_shape=(
-            jax.ShapeDtypeStruct((cx, cy, nz), jnp.float32),
-            jax.ShapeDtypeStruct((3, m, ny, nz), jnp.float32),
+            pltpu.VMEM((cx, cy, nz), jnp.float32),
+            pltpu.VMEM((3, m, ny, nz), jnp.float32),
         ),
         in_specs=[pl.BlockSpec(memory_space=pltpu.MemorySpace.HBM)] * 5,
-        out_specs=(pl.BlockSpec(memory_space=pltpu.MemorySpace.HBM),) * 2,
+        out_specs=(pl.BlockSpec(memory_space=pltpu.VMEM),) * 2,
         scratch_shapes=scratch,
         compiler_params=pltpu.CompilerParams(
             collective_id=0, has_side_effects=True, vmem_limit_bytes=61 * 2**20),

time: 42.4 us -> 39.1 us (0.922)
  local copies, waits for them, and re-layouts: 3.73 us -> 1.58 us
  Pallas kernels: 37.8 us -> 36.7 us
    unnamed x2, local copies, waits for them, and re-layouts: 3.73 us -> 1.58 us
    pallas_call x1, Pallas kernels: 37.8 us -> 36.7 us  [per_device(): pl.pallas_call(functools.partial(kernel, n_sx, n_sy), out_shape=(pltpu.VM...]
where the time goes in v3:
time: 39.1 us; the launch traced here: 39 us
  Pallas kernels  36.7 us (94%)
  local copies, waits for them, and re-layouts  1.58 us (4%)
  between operations  0.64 us (2%)
    pallas_call x1, Pallas kernels, per_device(): pl.pallas_call(functools.partial(kernel, n_sx, n_sy), out_shape=(pltpu.VM...  36.7 us
    unnamed x2, local copies, waits for them, and re-layouts  1.58 us

profile of v3, /device:TPU:0, one launch (start us, length us, event | category | flops | bytes accessed | tf_op | source)
XLA Modules:
  0.0 39.0 jit_solution(9982859528181328494)
XLA Ops:
  0.6 36.7 %shard_map.68 = (f32[32,16,128]{2,1,0:T(8,128)S(1)}, f32[3,4,128,128]{3,2,1,0:T(8,128)S(1)}) custom-call(f32[32,16,128]{2,1,0:T(8,128)} %right_hbm.1, s32[16,8,32]{2,1,0:T(8,128)} %class_hbm.1, f32[8]{0:T(128)} %table_hbm.1, f32[3,32,16,128]{3,2,1,0:T(8,128)} %velocity_ref.1, f32[128,128]{1,0:T(8,128)} %constant.2.clone.matrix_hbm), custom_call_target="tpu_custom_call" | custom-call | tf_op jit(solution)/shard_map/pallas_call | solution.py:531
  37.4 0.7 %copy.9 = f32[32,16,128]{2,1,0:T(8,128)} copy(f32[32,16,128]{2,1,0:T(8,128)S(1)} %get-tuple-element.2) | data formatting | bytes 524288
  38.1 0.9 %copy.10 = f32[3,4,128,128]{3,2,1,0:T(8,128)} copy(f32[3,4,128,128]{3,2,1,0:T(8,128)S(1)} %get-tuple-element.3) | data formatting | bytes 1572864

commit v4 on v3

--- a/solution.py
+++ b/solution.py
@@ -173,32 +173,27 @@
 
         return arrive, leave
 
-    def to_lines(number, source, target):
-        def rows(who):
-            return pl.ds(pl.multiple_of(who * cy, cy), cy)
-
+    def take(span, sem):
+        pltpu.make_async_copy(span, span, sem).wait()
+
+    def to_lines(number, source, target, span):
         def copy(other, sender):
             return pltpu.make_async_remote_copy(
-                src_ref=source(other), dst_ref=target(sender), send_sem=a2a_send.at[number, other],
-                recv_sem=a2a_recv.at[number, sender], device_id=(p, other), device_id_type=MESH,
+                src_ref=source(other), dst_ref=target(sender), send_sem=a2a_send.at[number],
+                recv_sem=a2a_recv.at[number], device_id=(p, other), device_id_type=MESH,
             )
 
         def begin(k, _):
             copy(lax.rem(q + k, n_sy), q).start()
             return 0
 
-        def finish(k, _):
-            other = lax.rem(q + k, n_sy)
-            copy(other, q).wait_send()
-            copy(other, other).wait_recv()
-            return 0
-
         lax.fori_loop(1, n_sy, begin, 0)
         own = pltpu.make_async_copy(source(q), target(q), local_sem.at[number])
         own.start()
 
         def complete():
-            lax.fori_loop(1, n_sy, finish, 0)
+            take(span, a2a_send.at[number])
+            take(span, a2a_recv.at[number])
             own.wait()
 
         return complete
@@ -216,9 +211,11 @@
         1, (right_ref.at[pl.ds(0, M)], right_ref.at[pl.ds(cx - M, M)]), (res_y.at[0], res_y.at[1]),
         [res_c.at[at] for at in range(4)], got_rx, got_ry, got_rc)
     lines_c = to_lines(
-        0, lambda s: blk.at[pl.ds((s * m) // 2, mb)], lambda s: line_c.at[:, half_lines(s), :])
+        0, lambda s: blk.at[pl.ds((s * m) // 2, mb)], lambda s: line_c.at[:, half_lines(s), :],
+        line_c.at[:, pl.ds(0, (n_sy - 1) * hy), :])
     lines_v = to_lines(
-        1, lambda s: velocity_ref.at[:, pl.ds(s * m, m)], lambda s: line_v.at[:, :, lines(s), :])
+        1, lambda s: velocity_ref.at[:, pl.ds(s * m, m)], lambda s: line_v.at[:, :, lines(s), :],
+        line_v.at[:, :, pl.ds(0, (n_sy - 1) * cy), :])
 
     blk_arrive()
     wide_blk[H : H + hx, H : H + hy, :] = blk[...]
@@ -348,7 +345,8 @@
         2, (image.at[pl.ds(0, M)], image.at[pl.ds(cx - M, M)]), (img_y.at[0], img_y.at[1]),
         [img_c.at[at] for at in range(4)], got_ix, got_iy, got_ic)
     lines_f = to_lines(
-        2, lambda s: first_own.at[pl.ds(s * m, m + 2)], lambda s: line_f.at[:, lines(s), :])
+        2, lambda s: first_own.at[pl.ds(s * m, m + 2)], lambda s: line_f.at[:, lines(s), :],
+        line_f.at[:, pl.ds(0, (n_sy - 1) * cy), :])
 
     loads[3].wait()
     matrix = matrix_ref[...]
@@ -361,14 +359,6 @@
         fine = (field - coarse.astype(jnp.float32)).astype(jnp.bfloat16)
         return jnp.dot(
             factors, jnp.concatenate([coarse, fine, coarse], axis=0), preferred_element_type=jnp.float32)
-
-    lines_v()
-    lines_c()
-    for row in range(m):
-        c, vx, vy = factor(row), line_v[0, row], line_v[1, row]
-        next_ref[0, row] = diffuse(vx - c * vx)
-        next_ref[1, row] = diffuse(vy - c * vy)
-        next_ref[2, row] = diffuse(line_v[2, row])
 
     img_arrive()
     assemble(image, got_ix, got_iy, got_ic)
@@ -378,9 +368,15 @@
     q_own[cx + 1] = jnp.zeros((cy, nz), jnp.float32)
     q_own[1 : cx + 1] = buf_q[M : M + cx, M : M + cy, :]
     lines_q = to_lines(
-        3, lambda s: q_own.at[pl.ds(s * m, m + 2)], lambda s: line_q.at[:, lines(s), :])
-    lines_f()
-    forces([line_f[row] for row in range(m + 2)], force_f)
+        3, lambda s: q_own.at[pl.ds(s * m, m + 2)], lambda s: line_q.at[:, lines(s), :],
+        line_q.at[:, pl.ds(0, (n_sy - 1) * cy), :])
+    lines_v()
+    lines_c()
+    for row in range(m):
+        c, vx, vy = factor(row), line_v[0, row], line_v[1, row]
+        next_ref[0, row] = diffuse(vx - c * vx)
+        next_ref[1, row] = diffuse(vy - c * vy)
+        next_ref[2, row] = diffuse(line_v[2, row])
     q_arrive()
     q_leave()
     place_faces(buf_q, None, got_qx, got_qy)
@@ -441,29 +437,27 @@
     def gather(axis_at, count, mine, slots, send, recv, device):
         def copy(other, sender):
             return pltpu.make_async_remote_copy(
-                src_ref=mine, dst_ref=slots.at[sender], send_sem=send.at[other],
-                recv_sem=recv.at[sender], device_id=device(other), device_id_type=MESH)
+                src_ref=mine, dst_ref=slots.at[sender], send_sem=send.at[0],
+                recv_sem=recv.at[0], device_id=device(other), device_id_type=MESH)
 
         def begin(k, _):
             copy(lax.rem(axis_at + k, count), axis_at).start()
             return 0
 
-        def finish(k, _):
-            other = lax.rem(axis_at + k, count)
-            copy(other, axis_at).wait_send()
-            copy(other, other).wait_recv()
-            return 0
-
         lax.fori_loop(1, count, begin, 0)
         slots[axis_at] = mine[...]
 
         def complete():
-            lax.fori_loop(1, count, finish, 0)
+            span = slots.at[pl.ds(0, count - 1)]
+            take(span, send.at[0])
+            take(span, recv.at[0])
             return jnp.sum(slots[...], axis=0)
 
         return complete
 
     row_sums = gather(p, n_sx, sums_mine, sums_x, sx_send, sx_recv, lambda other: (other, q))
+    lines_f()
+    forces([line_f[row] for row in range(m + 2)], force_f)
     sums_row[...] = row_sums()
     all_sums = gather(q, n_sy, sums_row, sums_y, sy_send, sy_recv, lambda other: (p, other))
     blk_leave()
@@ -524,8 +518,8 @@
         vmem(3, m, ny, nz), vmem(mb, ny // 2, nz), vmem(m + 2, ny, nz), vmem(m + 2, ny, nz),
         vmem(8, nz), vmem(n_sx, 8, nz), vmem(8, nz), vmem(n_sy, 8, nz),
         dma((3, 8)), dma((3, 8)), dma((2, 8)), dma((2, 8)),
-        dma((4, n_sy)), dma((4, n_sy)), dma((4,)),
-        dma((n_sx,)), dma((n_sx,)), dma((n_sy,)), dma((n_sy,)),
+        dma((4,)), dma((4,)), dma((4,)),
+        dma((1,)), dma((1,)), dma((1,)), dma((1,)),
         vmem(2, m, ny, nz), vmem(2, m, ny, nz), vmem(2, cy, nz), vmem(ny, nz), dma((2,)), dma((n_sy,)),
     ]
     return pl.pallas_call(

time: 39.1 us -> 38.2 us (0.977)
  Pallas kernels: 36.7 us -> 35.8 us
    pallas_call x1, Pallas kernels: 36.7 us -> 35.8 us  [per_device(): pl.pallas_call(functools.partial(kernel, n_sx, n_sy), out_shape=(pltpu.VM...]
where the time goes in v4:
time: 38.2 us; the launch traced here: 38 us
  Pallas kernels  35.8 us (94%)
  local copies, waits for them, and re-layouts  1.58 us (4%)
  between operations  0.64 us (2%)
    pallas_call x1, Pallas kernels, per_device(): pl.pallas_call(functools.partial(kernel, n_sx, n_sy), out_shape=(pltpu.VM...  35.8 us
    unnamed x2, local copies, waits for them, and re-layouts  1.58 us

profile of v4, /device:TPU:0, one launch (start us, length us, event | category | flops | bytes accessed | tf_op | source)
XLA Modules:
  0.0 38.0 jit_solution(12199964127358552891)
XLA Ops:
  0.6 35.8 %shard_map.68 = (f32[32,16,128]{2,1,0:T(8,128)S(1)}, f32[3,4,128,128]{3,2,1,0:T(8,128)S(1)}) custom-call(f32[32,16,128]{2,1,0:T(8,128)} %right_hbm.1, s32[16,8,32]{2,1,0:T(8,128)} %class_hbm.1, f32[8]{0:T(128)} %table_hbm.1, f32[3,32,16,128]{3,2,1,0:T(8,128)} %velocity_ref.1, f32[128,128]{1,0:T(8,128)} %constant.2.clone.matrix_hbm), custom_call_target="tpu_custom_call" | custom-call | tf_op jit(solution)/shard_map/pallas_call | solution.py:525
  36.4 0.7 %copy.9 = f32[32,16,128]{2,1,0:T(8,128)} copy(f32[32,16,128]{2,1,0:T(8,128)S(1)} %get-tuple-element.2) | data formatting | bytes 524288
  37.1 0.9 %copy.10 = f32[3,4,128,128]{3,2,1,0:T(8,128)} copy(f32[3,4,128,128]{3,2,1,0:T(8,128)S(1)} %get-tuple-element.3) | data formatting | bytes 1572864

commit v5 on v4

--- a/solution.py
+++ b/solution.py
@@ -213,9 +213,6 @@
     lines_c = to_lines(
         0, lambda s: blk.at[pl.ds((s * m) // 2, mb)], lambda s: line_c.at[:, half_lines(s), :],
         line_c.at[:, pl.ds(0, (n_sy - 1) * hy), :])
-    lines_v = to_lines(
-        1, lambda s: velocity_ref.at[:, pl.ds(s * m, m)], lambda s: line_v.at[:, :, lines(s), :],
-        line_v.at[:, :, pl.ds(0, (n_sy - 1) * cy), :])
 
     blk_arrive()
     wide_blk[H : H + hx, H : H + hy, :] = blk[...]
@@ -330,6 +327,9 @@
     assemble(right_ref, got_rx, got_ry, got_rc)
     precondition(buf_b)
     face_arrive, face_leave = send_faces(0, buf_b, first_y, got_fx, got_fy)
+    lines_v = to_lines(
+        1, lambda s: velocity_ref.at[:, pl.ds(s * m, m)], lambda s: line_v.at[:, :, lines(s), :],
+        line_v.at[:, :, pl.ds(0, (n_sy - 1) * cy), :])
     face_arrive()
     face_leave()
     place_faces(buf_b, first_own, got_fx, got_fy)

time: 38.2 us -> 38.5 us (level)
  no operation moved by 1% of the time
where the time goes in v5:
time: 38.5 us; the launch traced here: 38.4 us
  Pallas kernels  36.1 us (94%)
  local copies, waits for them, and re-layouts  1.58 us (4%)
  between operations  0.64 us (2%)
    pallas_call x1, Pallas kernels, per_device(): pl.pallas_call(functools.partial(kernel, n_sx, n_sy), out_shape=(pltpu.VM...  36.1 us
    unnamed x2, local copies, waits for them, and re-layouts  1.58 us

profile of v5, /device:TPU:0, one launch (start us, length us, event | category | flops | bytes accessed | tf_op | source)
XLA Modules:
  0.0 38.4 jit_solution(693924743137136316)
XLA Ops:
  0.6 36.1 %shard_map.68 = (f32[32,16,128]{2,1,0:T(8,128)S(1)}, f32[3,4,128,128]{3,2,1,0:T(8,128)S(1)}) custom-call(f32[32,16,128]{2,1,0:T(8,128)} %right_hbm.1, s32[16,8,32]{2,1,0:T(8,128)} %class_hbm.1, f32[8]{0:T(128)} %table_hbm.1, f32[3,32,16,128]{3,2,1,0:T(8,128)} %velocity_ref.1, f32[128,128]{1,0:T(8,128)} %constant.2.clone.matrix_hbm), custom_call_target="tpu_custom_call" | custom-call | tf_op jit(solution)/shard_map/pallas_call | solution.py:525
  36.8 0.7 %copy.9 = f32[32,16,128]{2,1,0:T(8,128)} copy(f32[32,16,128]{2,1,0:T(8,128)S(1)} %get-tuple-element.2) | data formatting | bytes 524288
  37.5 0.9 %copy.10 = f32[3,4,128,128]{3,2,1,0:T(8,128)} copy(f32[3,4,128,128]{3,2,1,0:T(8,128)S(1)} %get-tuple-element.3) | data formatting | bytes 1572864

commit v6 on v4

--- a/solution.py
+++ b/solution.py
@@ -360,6 +360,8 @@
         return jnp.dot(
             factors, jnp.concatenate([coarse, fine, coarse], axis=0), preferred_element_type=jnp.float32)
 
+    blk_leave()
+    res_leave()
     img_arrive()
     assemble(image, got_ix, got_iy, got_ic)
     precondition(buf_q)
@@ -377,6 +379,7 @@
         next_ref[0, row] = diffuse(vx - c * vx)
         next_ref[1, row] = diffuse(vy - c * vy)
         next_ref[2, row] = diffuse(line_v[2, row])
+    img_leave()
     q_arrive()
     q_leave()
     place_faces(buf_q, None, got_qx, got_qy)
@@ -460,9 +463,6 @@
     forces([line_f[row] for row in range(m + 2)], force_f)
     sums_row[...] = row_sums()
     all_sums = gather(q, n_sy, sums_row, sums_y, sy_send, sy_recv, lambda other: (p, other))
-    blk_leave()
-    res_leave()
-    img_leave()
     lines_q()
     edges()
     planes = [line_q[row] for row in range(m + 2)]

time: 38.2 us -> 38.2 us (level)
  no operation moved by 1% of the time
where the time goes in v6:
time: 38.2 us; the launch traced here: 38 us
  Pallas kernels  35.8 us (94%)
  local copies, waits for them, and re-layouts  1.58 us (4%)
  between operations  0.64 us (2%)
    pallas_call x1, Pallas kernels, per_device(): pl.pallas_call(functools.partial(kernel, n_sx, n_sy), out_shape=(pltpu.VM...  35.8 us
    unnamed x2, local copies, waits for them, and re-layouts  1.58 us

profile of v6, /device:TPU:0, one launch (start us, length us, event | category | flops | bytes accessed | tf_op | source)
XLA Modules:
  0.0 38.0 jit_solution(11395639540124696078)
XLA Ops:
  0.6 35.8 %shard_map.68 = (f32[32,16,128]{2,1,0:T(8,128)S(1)}, f32[3,4,128,128]{3,2,1,0:T(8,128)S(1)}) custom-call(f32[32,16,128]{2,1,0:T(8,128)} %right_hbm.1, s32[16,8,32]{2,1,0:T(8,128)} %class_hbm.1, f32[8]{0:T(128)} %table_hbm.1, f32[3,32,16,128]{3,2,1,0:T(8,128)} %velocity_ref.1, f32[128,128]{1,0:T(8,128)} %constant.2.clone.matrix_hbm), custom_call_target="tpu_custom_call" | custom-call | tf_op jit(solution)/shard_map/pallas_call | solution.py:525
  36.4 0.7 %copy.9 = f32[32,16,128]{2,1,0:T(8,128)} copy(f32[32,16,128]{2,1,0:T(8,128)S(1)} %get-tuple-element.2) | data formatting | bytes 524288
  37.1 0.9 %copy.10 = f32[3,4,128,128]{3,2,1,0:T(8,128)} copy(f32[3,4,128,128]{3,2,1,0:T(8,128)S(1)} %get-tuple-element.3) | data formatting | bytes 1572864
